TPU v7x, 128 devices: a whole 4x4x4 slice. The times are simulated.
128 devices in a mesh: wide: 32 (over y, z_lo, x), narrow: 4 (over z_hi, core).
Axes of the slice: x: 4, y: 4, z: 4 (z_hi: 2, z_lo: 2; z = z_hi * 2 + z_lo), core: 2. Of those that a mesh axis runs over, the one named last changes fastest.
Arguments:
- token_ids: int32 [2, 256], P(None, 'wide'), may hold values from 0 to 511
- lengths: int32 [256], P(('wide', 'narrow')), may hold values from 1 to 62, as said below
- embedding: bfloat16 [512, 8192], P(None, 'narrow'), may hold values from -6 to 6
- hyena_gain: float32 [8192], P('narrow'), may hold values from 0.1 to 1.9
- hyena_in: bfloat16 [8192, 3, 8192], P('narrow', None, 'wide'), may hold values from -0.0625 to 0.0625
- fir_taps: float32 [3, 3, 8192], P(None, None, 'wide'), may hold values from -3 to 3
- poles: float32 [16, 8192], P(None, 'wide'), may hold values from 0.3 to 0.995
- residues: float32 [16, 8192], P(None, 'wide'), may hold values from -2 to 2
- skip: float32 [8192], P('wide'), may hold values from 0.5 to 1.5
- hyena_out: bfloat16 [8192, 8192], P('wide', 'narrow'), may hold values from -0.0625 to 0.0625
- modal_state: float32 [256, 16, 8192], P('narrow', None, 'wide'), may hold values from -6 to 6
- fir_state: float32 [256, 2, 3, 8192], P('narrow', None, None, 'wide'), may hold values from -6 to 6
- attn_gain: float32 [8192], P('narrow'), may hold values from 0.1 to 1.9
- attn_in: bfloat16 [8192, 3, 8192], P('narrow', None, 'wide'), may hold values from -0.0625 to 0.0625
- attn_out: bfloat16 [8192, 8192], P('wide', 'narrow'), may hold values from -0.0625 to 0.0625
- kv_cache: bfloat16 [256, 64, 2, 8192], P(('wide', 'narrow')), may hold values from -512 to 512
Outputs:
- hidden_states: bfloat16 [2, 256, 8192], P(None, 'wide', 'narrow')
- modal_out: float32 [256, 16, 8192], P('narrow', None, 'wide')
- fir_out: float32 [256, 2, 3, 8192], P('narrow', None, None, 'wide')
Inputs may be any that keep to these rules, and one draw needn't show every extreme that they name: `lengths`: a sequence's cache holds valid keys at positions below its length; some sequence has length 62.
All inputs are finite; a program needn't handle non-finite values.
Results may differ from a plain program's by a relative error of at most 0.035.
Values may be sent and summed in bfloat16 or wider, within the bound.
A program may use at most 128 MiB of HBM per device.

v0:
```python
import math

import jax
import jax.numpy as jnp
from jax import lax
from jax.sharding import PartitionSpec as P

D = 8192
HEADS = 64
HEAD_DIM = 128
STEPS = 2


EPS = 1e-06


def norm_rows(hidden, gain):
    values = hidden.astype(jnp.float32)
    total = lax.psum(jnp.sum(values * values, axis=1), "narrow")
    return (values * lax.rsqrt(total / D + EPS)[:, None] * gain).astype(jnp.bfloat16)


def rotate(vectors, positions):
    half = HEAD_DIM // 2
    freqs = jnp.exp(-math.log(10000.0) * jnp.arange(half, dtype=jnp.float32) * 2.0 / HEAD_DIM)
    angles = positions.astype(jnp.float32)[:, None, None] * freqs[None, None, :]
    cosine = jnp.cos(angles)
    sine = jnp.sin(angles)
    first = vectors[..., :half]
    second = vectors[..., half:]
    return jnp.concatenate(
        [first * cosine - second * sine, second * cosine + first * sine], axis=-1
    )


def attend_local(query, cache, valid_len, fresh_keys, fresh_values):
    rows, span = (cache.shape[0], cache.shape[1])
    keys = cache[:, :, 0].reshape(rows, span, HEADS, HEAD_DIM)
    values = cache[:, :, 1].reshape(rows, span, HEADS, HEAD_DIM)
    scale = 1.0 / math.sqrt(HEAD_DIM)
    scores = jnp.einsum("bhd,blhd->bhl", query, keys, preferred_element_type=jnp.float32) * scale
    valid = jnp.arange(span, dtype=jnp.int32)[None, :] < valid_len[:, None]
    scores = jnp.where(valid[:, None, :], scores, -1e30)
    fresh = (
        jnp.einsum("bhd,bshd->bhs", query, fresh_keys, preferred_element_type=jnp.float32) * scale
    )
    top = jnp.maximum(jnp.max(scores, axis=2), jnp.max(fresh, axis=2))[:, :, None]
    cache_w = jnp.exp(scores - top)
    fresh_w = jnp.exp(fresh - top)
    total = jnp.sum(cache_w, axis=2, keepdims=True) + jnp.sum(fresh_w, axis=2, keepdims=True)
    cache_w = (cache_w / total).astype(jnp.bfloat16)
    fresh_w = (fresh_w / total).astype(jnp.bfloat16)
    summed = jnp.einsum("bhl,blhd->bhd", cache_w, values, preferred_element_type=jnp.float32)
    summed = summed + jnp.einsum(
        "bhs,bshd->bhd", fresh_w, fresh_values, preferred_element_type=jnp.float32
    )
    return summed.reshape(rows, HEADS * HEAD_DIM).astype(jnp.bfloat16)


def local(
    token_ids,
    lengths,
    embedding,
    hyena_gain,
    hyena_in,
    fir_taps,
    poles,
    residues,
    skip,
    hyena_out,
    modal_state,
    fir_state,
    attn_gain,
    attn_in,
    attn_out,
    kv_cache,
):
    wide_count = lax.axis_size("wide")
    narrow_count = lax.axis_size("narrow")
    rows_wide = token_ids.shape[1]
    rows_narrow = modal_state.shape[0]
    rows_local = kv_cache.shape[0]
    batch = rows_wide * wide_count
    channels = poles.shape[1]
    vocab = embedding.shape[0]
    in_matrix = hyena_in.reshape(hyena_in.shape[0], 3 * channels)
    qkv_matrix = attn_in.reshape(attn_in.shape[0], 3 * channels)
    modal = modal_state
    fir = fir_state
    kept_keys = []
    kept_values = []
    outputs = []
    for step in range(STEPS):
        onehot = (token_ids[step][:, None] == jnp.arange(vocab, dtype=jnp.int32)[None, :]).astype(
            jnp.bfloat16
        )
        hidden0 = jnp.dot(onehot, embedding, preferred_element_type=jnp.float32).astype(
            jnp.bfloat16
        )
        normed0 = norm_rows(hidden0, hyena_gain)
        z_part = jnp.dot(
            lax.all_gather(normed0, "wide", axis=0, tiled=True),
            in_matrix,
            preferred_element_type=jnp.float32,
        )
        projected = (
            lax.psum_scatter(z_part.astype(jnp.bfloat16), "narrow", scatter_dimension=0, tiled=True)
            .astype(jnp.float32)
            .reshape(rows_narrow, 3, channels)
        )
        filtered = fir_taps[0] * projected + fir_taps[1] * fir[:, 0] + fir_taps[2] * fir[:, 1]
        fir = jnp.stack([projected, fir[:, 0]], axis=1)
        gated = filtered[:, 1] * filtered[:, 2]
        modal = poles * modal + gated[:, None, :]
        mixed = jnp.sum(residues * modal, axis=1) + skip * gated
        mixer = (filtered[:, 0] * mixed).astype(jnp.bfloat16)
        mixer_all = lax.all_gather(mixer, "narrow", axis=0, tiled=True)
        branch = lax.psum_scatter(
            jnp.dot(mixer_all, hyena_out, preferred_element_type=jnp.float32).astype(jnp.bfloat16),
            "wide",
            scatter_dimension=0,
            tiled=True,
        ).astype(jnp.float32)
        hidden1 = (hidden0.astype(jnp.float32) + branch).astype(jnp.bfloat16)
        normed1 = norm_rows(hidden1, attn_gain)
        qkv_part = jnp.dot(
            lax.all_gather(normed1, "wide", axis=0, tiled=True),
            qkv_matrix,
            preferred_element_type=jnp.float32,
        )
        blocks = qkv_part.reshape(wide_count, narrow_count, rows_local, 3 * channels)
        qkv_rows = lax.psum_scatter(
            blocks.astype(jnp.bfloat16), "narrow", scatter_dimension=1, tiled=True
        ).astype(jnp.float32)
        qkv_rows = qkv_rows.astype(jnp.bfloat16).reshape(wide_count, rows_local, 3, channels)
        local_qkv = lax.all_to_all(qkv_rows, "wide", split_axis=0, concat_axis=3, tiled=True)
        local_qkv = local_qkv.reshape(rows_local, 3, HEADS, HEAD_DIM)
        positions = lengths + step
        query = rotate(local_qkv[:, 0].astype(jnp.float32), positions).astype(jnp.bfloat16)
        key = rotate(local_qkv[:, 1].astype(jnp.float32), positions).astype(jnp.bfloat16)
        kept_keys.append(key)
        kept_values.append(local_qkv[:, 2])
        attended = attend_local(
            query, kv_cache, lengths, jnp.stack(kept_keys, axis=1), jnp.stack(kept_values, axis=1)
        )
        pieces = attended.reshape(rows_local, wide_count, channels)
        moved = lax.all_to_all(pieces, "wide", split_axis=1, concat_axis=0, tiled=True)
        moved = moved.reshape(wide_count, 1, rows_local, channels)
        attended_all = lax.all_gather(moved, "narrow", axis=1, tiled=True).reshape(batch, channels)
        branch2 = lax.psum_scatter(
            jnp.dot(attended_all, attn_out, preferred_element_type=jnp.float32).astype(
                jnp.bfloat16
            ),
            "wide",
            scatter_dimension=0,
            tiled=True,
        ).astype(jnp.float32)
        outputs.append((hidden1.astype(jnp.float32) + branch2).astype(jnp.bfloat16))
    return (jnp.stack(outputs), modal, fir)


def solution(mesh):
    placed = (
        P(None, "wide"),
        P(("wide", "narrow")),
        P(None, "narrow"),
        P("narrow"),
        P("narrow", None, "wide"),
        P(None, None, "wide"),
        P(None, "wide"),
        P(None, "wide"),
        P("wide"),
        P("wide", "narrow"),
        P("narrow", None, "wide"),
        P("narrow", None, None, "wide"),
        P("narrow"),
        P("narrow", None, "wide"),
        P("wide", "narrow"),
        P(("wide", "narrow"), None, None, None),
    )
    return jax.shard_map(
        local,
        mesh=mesh,
        in_specs=placed,
        out_specs=(
            P(None, "wide", "narrow"),
            P("narrow", None, "wide"),
            P("narrow", None, None, "wide"),
        ),
        check_vma=False,
    )
```

profile of v0, /device:TPU:0, one launch (start us, length us, event | category | flops | bytes accessed | tf_op | source)
XLA Modules:
  0.0 1458.7 jit_solution(1596795826157232248)
XLA Ops:
  9.9 10.9 all-reduce.1
  22.3 4.7 copy.158
  27.0 145.0 %all-gather.7.cloned.1.call-done = bf16[256,2048]{1,0:T(8,128)(2,1)} async-done(((bf16[8,2048]{1,0:T(8,128)(2,1)}), bf16[256,2048]{1,0:T(8,128)(2,1)}) %all-gather.7.cloned.1.call-update) | async-done | bytes 1048592 | tf_op jit(solution)/shard_map/all_gather | solution.py:102
  176.0 149.2 %all-gather.11.cloned.1.call-done = bf16[256,2048]{1,0:T(8,128)(2,1)} async-done(((bf16[8,2048]{1,0:T(8,128)(2,1)}), bf16[256,2048]{1,0:T(8,128)(2,1)}) %all-gather.11.cloned.1.call-update) | async-done | bytes 1048592 | tf_op jit(solution)/shard_map/all_gather | solution.py:102
  330.9 25.5 %reduce-scatter.9.cloned.1.call-done = bf16[64,768]{1,0:T(8,128)(2,1)} async-done(((bf16[256,768]{1,0:T(8,128)(2,1)}), bf16[64,768]{1,0:T(8,128)(2,1)}) %reduce-scatter.9.cloned.1.call-update) | async-done | bytes 98320 | tf_op jit(solution)/shard_map/reduce_scatter | solution.py:107
  357.3 29.2 %reduce-scatter.17.cloned.1.call-done = bf16[64,768]{1,0:T(8,128)(2,1)} async-done(((bf16[256,768]{1,0:T(8,128)(2,1)}), bf16[64,768]{1,0:T(8,128)(2,1)}) %reduce-scatter.17.cloned.1.call-update) | async-done | bytes 98320 | tf_op jit(solution)/shard_map/reduce_scatter | solution.py:107
  391.3 6.9 all_gather.29
  399.8 6.9 all_gather.25
  408.2 151.7 %reduce-scatter.19.cloned.1.call-done = bf16[8,2048]{1,0:T(8,128)(2,1)} async-done(((bf16[256,2048]{1,0:T(8,128)(2,1)}), bf16[8,2048]{1,0:T(8,128)(2,1)}) %reduce-scatter.19.cloned.1.call-update) | async-done | bytes 32784 | tf_op jit(solution)/shard_map/reduce_scatter | solution.py:118
  560.8 158.4 %reduce-scatter.11.cloned.1.call-done = bf16[8,2048]{1,0:T(8,128)(2,1)} async-done(((bf16[256,2048]{1,0:T(8,128)(2,1)}), bf16[8,2048]{1,0:T(8,128)(2,1)}) %reduce-scatter.11.cloned.1.call-update) | async-done | bytes 32784 | tf_op jit(solution)/shard_map/reduce_scatter | solution.py:118
  720.0 7.2 all-reduce
  733.4 141.7 %all-gather.13.cloned.1.call-done = bf16[256,2048]{1,0:T(8,128)(2,1)} async-done(((bf16[8,2048]{1,0:T(8,128)(2,1)}), bf16[256,2048]{1,0:T(8,128)(2,1)}) %all-gather.13.cloned.1.call-update) | async-done | bytes 1048592 | tf_op jit(solution)/shard_map/all_gather | solution.py:127
  881.3 147.1 %all-gather.9.cloned.1.call-done = bf16[256,2048]{1,0:T(8,128)(2,1)} async-done(((bf16[8,2048]{1,0:T(8,128)(2,1)}), bf16[256,2048]{1,0:T(8,128)(2,1)}) %all-gather.9.cloned.1.call-update) | async-done | bytes 1048592 | tf_op jit(solution)/shard_map/all_gather | solution.py:127
  1034.4 21.9 %slice_reduce_fusion.1 = (bf16[2,64,8192]{2,1,0:T(8,128)(2,1)}, bf16[2,64,8192]{2,1,0:T(8,128)(2,1)}) fusion(bf16[2,64,2,8192]{3,2,1,0:T(2,128)(2,1)} %param.31), kind=kLoop, calls=%fused_computation.1 | loop fusion | bytes 8388608 | tf_op jit(solution)/shard_map/slice | solution.py:38
  1060.7 7.2 all-to-all-start.2
  1068.0 21.2 %reduce-scatter.13.cloned.1.call-done = bf16[32,1,2,768]{3,0,2,1:T(8,128)(2,1)} async-done(((bf16[32,4,2,768]{3,0,2,1:T(8,128)(2,1)}), bf16[32,1,2,768]{3,0,2,1:T(8,128)(2,1)}) %reduce-scatter.13.cloned.1.call-update) | async-done | bytes 98320 | tf_op jit(solution)/shard_map/reduce_scatter | solution.py:132
  1090.9 7.2 all-to-all-start
  1098.2 8.5 all-to-all-done
  1113.4 11.8 all_to_all.60
  1125.2 6.9 all-gather
  1136.6 11.7 all_to_all.61
  1148.3 6.9 all-gather.1
  1158.1 132.8 %reduce-scatter.15.cloned.1.call-done = bf16[8,2048]{1,0:T(8,128)(2,1)} async-done(((bf16[256,2048]{1,0:T(8,128)(2,1)}), bf16[8,2048]{1,0:T(8,128)(2,1)}) %reduce-scatter.15.cloned.1.call-update) | async-done | bytes 32784 | tf_op jit(solution)/shard_map/reduce_scatter | solution.py:150
  1291.7 158.8 %reduce-scatter.23.cloned.1.call-done = bf16[8,2048]{1,0:T(8,128)(2,1)} async-done(((bf16[256,2048]{1,0:T(8,128)(2,1)}), bf16[8,2048]{1,0:T(8,128)(2,1)}) %reduce-scatter.23.cloned.1.call-update) | async-done | bytes 32784 | tf_op jit(solution)/shard_map/reduce_scatter | solution.py:150
  (147 shorter events, 64.7 us)
Async XLA Ops:
  7.2 164.8 %all-gather.7.cloned.1.call-start = ((), (), s32[]{:S(2)}) async-start(), calls=%async_computation.12 | async-start | bytes 1081344 | tf_op jit(solution)/shard_map/all_gather | solution.py:102
  21.5 303.7 %all-gather.11.cloned.1.call-start = ((), (), s32[]{:S(2)}) async-start(), calls=%async_computation.18 | async-start | bytes 1081344 | tf_op jit(solution)/shard_map/all_gather | solution.py:102
  22.2 334.2 %reduce-scatter.9.cloned.1.call-start = ((), (), s32[]{:S(2)}) async-start(), calls=%async_computation.13 | async-start | bytes 491520 | tf_op jit(solution)/shard_map/reduce_scatter | solution.py:107
  175.9 153.3 %copy-start.13 = (f32[3,3,256]{2,1,0:T(4,128)S(1)}, f32[3,3,256]{2,1,0:T(4,128)}, u32[]{:S(2)}) copy-start(f32[3,3,256]{2,1,0:T(4,128)} %param.21) | copy-start | bytes 27652
  176.0 153.9 %copy-start.9 = (f32[64,2,3,256]{3,1,2,0:T(2,128)S(1)}, f32[64,2,3,256]{3,1,2,0:T(2,128)}, u32[]{:S(2)}) copy-start(f32[64,2,3,256]{3,1,2,0:T(2,128)} %param.27) | copy-start | bytes 1179652
  176.0 210.6 %reduce-scatter.17.cloned.1.call-start = ((), (), s32[]{:S(2)}) async-start(), calls=%async_computation.19 | async-start | bytes 491520 | tf_op jit(solution)/shard_map/reduce_scatter | solution.py:107
  329.2 59.4 %copy-start.12 = (f32[16,256]{1,0:T(8,128)S(1)}, f32[16,256]{1,0:T(8,128)}, u32[]{:S(2)}) copy-start(f32[16,256]{1,0:T(8,128)} %param.22) | copy-start | bytes 49156
  329.2 230.6 %reduce-scatter.19.cloned.1.call-start = ((), (), s32[]{:S(2)}) async-start(), calls=%async_computation.20 | async-start | bytes 1081344 | tf_op jit(solution)/shard_map/reduce_scatter | solution.py:118
  399.7 160.2 %copy-start.8 = (f32[8,2048]{1,0:T(8,128)S(1)}, f32[8,2048]{1,0:T(8,128)}, u32[]{:S(2)}) copy-start(f32[8,2048]{1,0:T(8,128)} %copy-done.7) | copy-start | bytes 196612
  399.7 319.4 %copy-start.6 = (f32[8,2048]{1,0:T(8,128)S(1)}, f32[8,2048]{1,0:T(8,128)}, u32[]{:S(2)}) copy-start(f32[8,2048]{1,0:T(8,128)} %copy-done.5) | copy-start | bytes 196612
  399.7 327.5 %copy-start.15 = (f32[2048]{0:T(1024)S(1)}, f32[2048]{0:T(1024)}, u32[]{:S(2)}) copy-start(f32[2048]{0:T(1024)} %param.28) | copy-start | bytes 24580
  399.7 319.4 %reduce-scatter.11.cloned.1.call-start = ((), (), s32[]{:S(2)}) async-start(), calls=%async_computation.14 | async-start | bytes 1081344 | tf_op jit(solution)/shard_map/reduce_scatter | solution.py:118
  408.1 467.0 %all-gather.13.cloned.1.call-start = ((), (), s32[]{:S(2)}) async-start(), calls=%async_computation.21 | async-start | bytes 1081344 | tf_op jit(solution)/shard_map/all_gather | solution.py:127
  727.9 300.5 %all-gather.9.cloned.1.call-start = ((), (), s32[]{:S(2)}) async-start(), calls=%async_computation.15 | async-start | bytes 1081344 | tf_op jit(solution)/shard_map/all_gather | solution.py:127
  728.7 330.4 %reduce-scatter.21.cloned.1.call-start = ((), (), s32[]{:S(2)}) async-start(), calls=%async_computation.22 | async-start | bytes 491520 | tf_op jit(solution)/shard_map/reduce_scatter | solution.py:132
  881.1 208.1 %reduce-scatter.13.cloned.1.call-start = ((), (), s32[]{:S(2)}) async-start(), calls=%async_computation.16 | async-start | bytes 491520 | tf_op jit(solution)/shard_map/reduce_scatter | solution.py:132
  1034.3 22.0 %copy-start.17 = (s32[2]{0:T(128)S(1)}, s32[2]{0:T(128)}, u32[]{:S(2)}) copy-start(s32[2]{0:T(128)} %param.17) | copy-start | bytes 28
  1060.7 30.2 %all-to-all-start.2 = ((bf16[32,2,3,256]{3,1,2,0:T(2,128)(2,1)}), bf16[32,2,3,256]{3,1,2,0:T(2,128)(2,1)S(1)}, u32[]{:S(2)}, u32[]{:S(2)}) async-start(bf16[32,2,3,256]{3,1,2,0:T(2,128)(2,1)} %copy.175), calls=%async_computation.9 | async-start | bytes 196608 | tf_op jit(solution)/shard_map/all_to_all | solution.py:136
  1090.9 15.8 %all-to-all-start = ((bf16[32,2,3,256]{3,1,2,0:T(2,128)(2,1)}), bf16[32,2,3,256]{3,1,2,0:T(2,128)(2,1)S(1)}, u32[]{:S(2)}, u32[]{:S(2)}) async-start(bf16[32,2,3,256]{3,1,2,0:T(2,128)(2,1)} %copy.165), calls=%async_computation.3 | async-start | bytes 196608 | tf_op jit(solution)/shard_map/all_to_all | solution.py:136
  1098.1 192.8 %reduce-scatter.15.cloned.1.call-start = ((), (), s32[]{:S(2)}) async-start(), calls=%async_computation.17 | async-start | bytes 1081344 | tf_op jit(solution)/shard_map/reduce_scatter | solution.py:150
  1112.0 20.1 %copy-start.2 = (bf16[256,2048]{1,0:T(8,128)(2,1)S(1)}, bf16[256,2048]{1,0:T(8,128)(2,1)}, u32[]{:S(2)}) copy-start(bf16[256,2048]{1,0:T(8,128)(2,1)} %param.30) | copy-start | bytes 3145732
  1133.6 316.9 %reduce-scatter.23.cloned.1.call-start = ((), (), s32[]{:S(2)}) async-start(), calls=%async_computation.23 | async-start | bytes 1081344 | tf_op jit(solution)/shard_map/reduce_scatter | solution.py:150
  1136.5 20.2 %copy-start.11 = (bf16[64,768]{1,0:T(8,128)(2,1)S(1)}, bf16[64,768]{1,0:T(8,128)(2,1)}, u32[]{:S(2)}) copy-start(bf16[64,768]{1,0:T(8,128)(2,1)} %reduce-scatter.17.cloned.1.call-done) | copy-start | bytes 294916
  1136.5 20.3 %copy-start.10 = (bf16[64,768]{1,0:T(8,128)(2,1)S(1)}, bf16[64,768]{1,0:T(8,128)(2,1)}, u32[]{:S(2)}) copy-start(bf16[64,768]{1,0:T(8,128)(2,1)} %reduce-scatter.9.cloned.1.call-done) | copy-start | bytes 294916
  (8 other events, 71.4 us)
Sparse Core Ops, SparseCore 0:
  21.6 150.2 all-gather.6
  174.2 151.0 all-gather.10
  328.4 27.9 reduce-scatter.8
  359.4 27.0 reduce-scatter.16
  399.8 159.9 reduce-scatter.18
  562.2 156.8 reduce-scatter.10
  728.1 147.0 all-gather.12
  877.4 151.0 all-gather.8
  1031.0 27.9 reduce-scatter.20
  1062.1 27.0 reduce-scatter.12
  1133.7 157.1 reduce-scatter.14
  1293.2 157.1 reduce-scatter.22
where the time goes:
time: 1460 us
  waiting for transfers between devices  1270 us (87%)
  blocking collectives  69.2 us (5%)
  local copies, waits for them, and re-layouts  43.1 us (3%)
  matrix products  30.6 us (2%)
  starting transfers between devices  15.1 us (1%)
  between operations  14.7 us (1%)
    reduce_scatter x2, waiting for transfers between devices, local(): lax.psum_scatter(jnp.dot(mixer_all, hyena_out, preferred_element_type=jnp...  310 us
    all_gather x2, waiting for transfers between devices, local(): lax.all_gather(normed0, 'wide', axis=0, tiled=True)  294 us
    reduce_scatter x2, waiting for transfers between devices, local(): lax.psum_scatter(jnp.dot(attended_all, attn_out, preferred_element_type=j...  292 us
    all_gather x2, waiting for transfers between devices, local(): lax.all_gather(normed1, 'wide', axis=0, tiled=True)  289 us
    reduce_scatter x2, waiting for transfers between devices, local(): lax.psum_scatter(z_part.astype(jnp.bfloat16), 'narrow', scatter_dimension...  54.8 us
  transfers between devices with their start and end apart: 14, of which 13 were waited for; matrix products, arithmetic and copies ran while one was open for 5% of the time, Pallas kernels for 0%

commit v1 on v0

v1 whole, which is shorter than its diff:
```python
import math

import jax
import jax.numpy as jnp
from jax import lax
from jax.experimental import pallas as pl
from jax.experimental.pallas import tpu as pltpu
from jax.sharding import PartitionSpec as P

D = 8192
HEADS = 64
HEAD_DIM = 128
STEPS = 2
EPS = 1e-06
MESH = pl.DeviceIdType.MESH
F32 = jnp.float32
BF16 = jnp.bfloat16
HALF = 1024


def dot(a, b):
    return jnp.dot(a, b, preferred_element_type=F32)


def dot_t(a, b):
    return lax.dot_general(a, b, (((1,), (1,)), ((), ())), preferred_element_type=F32)


class Place:
    def __init__(self):
        self.w = lax.axis_index("wide")
        self.n = lax.axis_index("narrow")
        self.y = self.w // 8
        self.zl = (self.w // 4) % 2
        self.x = self.w % 4
        self.zh = self.n // 2
        self.c = self.n % 2

    def along(self, axis, step):
        y = (self.y + step) % 4 if axis == "y" else self.y
        x = (self.x + step) % 4 if axis == "x" else self.x
        zl = (self.zl + step) % 2 if axis == "zl" else self.zl
        return ((y * 2 + zl) * 4 + x, self.n)

    def narrow(self, dzh, dc):
        return (self.w, ((self.zh + dzh) % 2) * 2 + (self.c + dc) % 2)


class Sems:
    def __init__(self, send, recv):
        self.send, self.recv, self.next = send, recv, 0

    def take(self, count=1):
        first = self.next
        self.next += count
        return first

    def copy(self, src, dst, device, slot=None):
        slot = self.take() if slot is None else slot
        made = pltpu.make_async_remote_copy(
            src_ref=src,
            dst_ref=dst,
            send_sem=self.send.at[slot],
            recv_sem=self.recv.at[slot],
            device_id=device,
            device_id_type=MESH,
        )
        made.start()
        return made


def add_blocks(out, terms, blocks):
    def body(k, carry):
        total = terms[0][k].astype(F32)
        for term in terms[1:]:
            total = total + term[k].astype(F32)
        out[k] = total.astype(out.dtype)
        return carry

    lax.fori_loop(0, blocks, body, 0)


def ring_rs(place, sems, axis, me, src, recv, temp, sink, blocks):
    sent = []
    first = []
    second = []
    for s, step in enumerate((1, 3)):
        there = place.along(axis, step)
        first.append(sems.copy(src.at[(me + 2) % 4, s], recv.at[s, 0], there))
        second.append(sems.copy(src.at[(me + step) % 4, 1 - s], recv.at[s, 1], there))
    yield
    third = []
    for s, step in enumerate((1, 3)):
        there = place.along(axis, step)
        first[s].wait_recv()
        add_blocks(temp.at[s], [src.at[(me + step) % 4, s], recv.at[s, 0]], blocks)
        third.append(sems.copy(temp.at[s], recv.at[s, 2], there))
    yield
    for z in range(2):
        second[1 - z].wait_recv()
        third[z].wait_recv()
        sink(z, [src.at[me, z], recv.at[z, 2], recv.at[1 - z, 1]])
    sent = first + second + third
    yield sent


def rs_wide_part(place, sems, axes, src, bufs, out):
    recv1, temp1, mid, recv2, temp2, last, recv3 = bufs
    sent = []

    def sink1(z, terms):
        def body(q, carry):
            total = terms[0][q].astype(F32)
            for term in terms[1:]:
                total = total + term[q].astype(F32)
            mid[q, z, 0] = total.astype(BF16)
            return carry

        lax.fori_loop(0, 4, body, 0)

    def sink2(z, terms):
        total = terms[0][0].astype(F32)
        for term in terms[1:]:
            total = total + term[0].astype(F32)
        last[z] = total.astype(BF16)

    for got in ring_rs(place, sems, axes[0], getattr(place, axes[0]), src, recv1, temp1, sink1, 4):
        if got is not None:
            sent += got
        else:
            yield
    for got in ring_rs(place, sems, axes[1], getattr(place, axes[1]), mid, recv2, temp2, sink2, 1):
        if got is not None:
            sent += got
        else:
            yield
    cross = sems.copy(last.at[1 - place.zl], recv3, place.along("zl", 1))
    yield
    cross.wait_recv()
    out(last[place.zl].astype(F32) + recv3[...].astype(F32))
    for copy in sent + [cross]:
        copy.wait_send()


def ag_wide_part(place, sems, axes, held):
    first, second = axes
    f, s, zl = getattr(place, first), getattr(place, second), place.zl
    sent = []
    own = held.at[f, zl, s]
    base = sems.take(4)
    near = []
    cross = sems.copy(own, own, place.along("zl", 1))
    for d, step in enumerate((1, 3)):
        sems.copy(own, own, place.along(second, step), base + d * 2 + zl)
    yield
    cross.wait_recv()
    other = held.at[f, 1 - zl, s]
    for d, step in enumerate((1, 3)):
        sems.copy(other, other, place.along(second, step), base + d * 2 + 1 - zl)
    for d, step in enumerate((1, 3)):
        for z in range(2):
            block = held.at[f, z, s]
            near.append(
                pltpu.make_async_remote_copy(
                    src_ref=block,
                    dst_ref=block,
                    send_sem=sems.send.at[base + d * 2 + z],
                    recv_sem=sems.recv.at[base + d * 2 + z],
                    device_id=place.along(second, step),
                    device_id_type=MESH,
                )
            )
    yield
    far = []
    for d, step in enumerate((1, 3)):
        near[d * 2 + d].wait_recv()
        block = held.at[f, d, (s - step) % 4]
        far.append(sems.copy(block, block, place.along(second, step)))
    yield
    near[1].wait_recv()
    near[2].wait_recv()
    far[0].wait_recv()
    far[1].wait_recv()
    near2 = []
    for z in range(2):
        for d, step in enumerate((1, 3)):
            block = held.at[f, z]
            near2.append(sems.copy(block, block, place.along(first, step)))
    yield
    far2 = []
    for d, step in enumerate((1, 3)):
        near2[d * 2 + d].wait_recv()
        block = held.at[(f - step) % 4, d]
        far2.append(sems.copy(block, block, place.along(first, step)))
    yield
    near2[1].wait_recv()
    near2[2].wait_recv()
    far2[0].wait_recv()
    far2[1].wait_recv()
    for copy in [cross] + near + far + near2 + far2:
        copy.wait_send()


def interleave(*parts):
    parts = list(parts)
    while parts:
        left = []
        for part in parts:
            try:
                next(part)
                left.append(part)
            except StopIteration:
                pass
        parts = left


def rs_narrow(place, sems, src, core_recv, temp, z_recv):
    zh, c = place.zh, place.c
    mate = place.narrow(0, 1)
    far = sems.copy(src.at[(1 - zh) * 2 + 1 - c], core_recv.at[0], mate)
    near = sems.copy(src.at[zh * 2 + 1 - c], core_recv.at[1], mate)
    far.wait_recv()
    add_blocks(temp, [src.at[(1 - zh) * 2 + c], core_recv.at[0]], temp.shape[0])
    cross = sems.copy(temp, z_recv, place.narrow(1, 0))
    near.wait_recv()
    cross.wait_recv()
    for copy in (far, near, cross):
        copy.wait_send()
    return [src.at[zh * 2 + c], core_recv.at[1], z_recv]


def ag_narrow(place, sems, held):
    zh, c = place.zh, place.c
    own = held.at[place.n]
    cross = sems.copy(own, own, place.narrow(1, 0))
    near = sems.copy(own, own, place.narrow(0, 1))
    cross.wait_recv()
    got = held.at[(1 - zh) * 2 + c]
    handed = sems.copy(got, got, place.narrow(0, 1))
    near.wait_recv()
    handed.wait_recv()
    for copy in (cross, near, handed):
        copy.wait_send()


def all_to_all(place, sems, src, dst):
    base = sems.take(32)

    def copy_of(d):
        peer = (place.w + d) % 32
        return pltpu.make_async_remote_copy(
            src_ref=src.at[peer],
            dst_ref=dst.at[place.w],
            send_sem=sems.send.at[base + d],
            recv_sem=sems.recv.at[base + d],
            device_id=(peer, place.n),
            device_id_type=MESH,
        )

    def begin(d, carry):
        copy_of(d).start()
        return carry

    def end(d, carry):
        copy_of(d).wait()
        return carry

    lax.fori_loop(1, 32, begin, 0)
    dst[place.w] = src[place.w]
    return lambda: lax.fori_loop(1, 32, end, 0)


def share_scales(place, sems, sums, got, scales):
    copies = []
    for k, (dzh, dc) in enumerate(((0, 1), (1, 0), (1, 1))):
        copies.append(sems.copy(sums, got.at[k], place.narrow(dzh, dc)))

    def finish():
        for copy in copies:
            copy.wait()
        total = sums[...] + got[0] + got[1] + got[2]
        scales[...] = lax.rsqrt(total / D + EPS)

    return finish


def project_out(rows, weights, parts):
    def body(y, carry):
        block = rows[pl.ds(pl.multiple_of(y * 128, 128), 128), :]
        a = dot(block, weights[:, :HALF]).astype(BF16).reshape(2, 4, 16, HALF)
        parts[0][y] = a
        b = dot(block, weights[:, HALF:]).astype(BF16).reshape(2, 4, 16, HALF)
        for x in range(4):
            parts[1][x, :, y] = b[:, x]
        return carry

    lax.fori_loop(0, 4, body, 0)


def kernel(
    tok_ref,
    hyena_gain_ref,
    attn_gain_ref,
    taps_ref,
    poles_ref,
    residues_ref,
    skip_ref,
    fir_ref,
    cos_ref,
    sin_ref,
    len_ref,
    emb_hbm,
    hyena_in_hbm,
    modal_hbm,
    hyena_out_hbm,
    attn_in_hbm,
    attn_out_hbm,
    kv_hbm,
    out_ref,
    modal_out_hbm,
    fir_out_ref,
    emb,
    hyena_in,
    modal,
    hyena_out,
    attn_in,
    attn_out,
    kv_raw,
    load_sem,
    send_sem,
    recv_sem,
    tokens,
    xg,
    table,
    zsend,
    zcore,
    ztemp,
    zrecv,
    sums,
    sums_got,
    scales,
    mixers,
    psend,
    r1,
    t1,
    m1,
    r2,
    t2,
    l2,
    r3,
    hidden0,
    hidden1,
    held,
    qkv,
    spread,
    spread16,
    routed,
    att_send,
    att_recv,
    att_rows,
    att_full,
):
    place = Place()
    sems = Sems(send_sem, recv_sem)
    w, n = place.w, place.n

    barrier = pltpu.get_barrier_semaphore()

    def greet(d, carry):
        pl.semaphore_signal(
            barrier, inc=1, device_id=((w + d) % 32, n), device_id_type=MESH
        )
        return carry

    lax.fori_loop(1, 32, greet, 0)
    for dzh, dc in ((0, 1), (1, 0), (1, 1)):
        pl.semaphore_signal(barrier, inc=1, device_id=place.narrow(dzh, dc), device_id_type=MESH)

    loads = []
    for k, (src, dst) in enumerate(
        (
            (emb_hbm, emb),
            (hyena_in_hbm, hyena_in),
            (modal_hbm, modal),
            (hyena_out_hbm, hyena_out),
            (attn_in_hbm, attn_in),
            (attn_out_hbm, attn_out),
        )
    ):
        copy = pltpu.make_async_copy(src, dst, load_sem.at[k])
        copy.start()
        loads.append(copy)

    loads[0].wait()

    def gain_rows(k, carry):
        rows = pl.ds(pl.multiple_of(k * 64, 64), 64)
        xg[rows, :] = (emb[rows, :].astype(F32) * hyena_gain_ref[...]).astype(BF16)
        return carry

    lax.fori_loop(0, 8, gain_rows, 0)
    sums[0] = dot_t(jnp.ones((8, 2048), BF16), emb[...] * emb[...])

    pl.semaphore_wait(barrier, 34)

    tokens[w] = tok_ref[...]
    base = sems.take(32)

    def token_copy(d):
        return pltpu.make_async_remote_copy(
            src_ref=tok_ref,
            dst_ref=tokens.at[w],
            send_sem=send_sem.at[base + d],
            recv_sem=recv_sem.at[base + d],
            device_id=((w + d) % 32, n),
            device_id_type=MESH,
        )

    def token_start(d, carry):
        token_copy(d).start()
        return carry

    def token_wait(d, carry):
        token_copy(d).wait()
        return carry

    lax.fori_loop(1, 32, token_start, 0)
    scales_ready = share_scales(place, sems, sums.at[0], sums_got.at[0], scales.at[0])

    def load_kv(h, carry):
        for j in range(2):
            lanes = pl.ds(pl.multiple_of(h * 128, 128), 128)
            pltpu.make_async_copy(kv_hbm.at[j, :, :, lanes], kv_raw.at[j, h], load_sem.at[6]).start()
        return carry

    loads[1].wait()
    lax.fori_loop(0, 64, load_kv, 0)

    def project(k, carry):
        c, m = k // 2, k % 2
        rows = pl.ds(pl.multiple_of(m * 256, 256), 256)
        table[c, rows, :] = dot(xg[rows, :], hyena_in[c]).astype(BF16)
        return carry

    lax.fori_loop(0, 6, project, 0)

    lax.fori_loop(1, 32, token_wait, 0)
    token_rows = tokens[...].reshape(256, 128)
    vocab = lax.broadcasted_iota(jnp.int32, (64, 512), 1)
    for t in range(STEPS):
        for m in range(4):
            hot = (token_rows[m * 64 : (m + 1) * 64, t * 64 : t * 64 + 1] == vocab).astype(F32).astype(BF16)
            for c in range(3):
                picked = dot(hot, table[c])
                zsend[m, t * 4 : t * 4 + 4, :, c * 256 : (c + 1) * 256] = picked.astype(BF16).reshape(
                    4, 16, 256
                )

    terms = rs_narrow(place, sems, zsend, zcore.at[0], ztemp.at[0], zrecv.at[0])
    scales_ready()

    mine = jnp.concatenate([tok_ref[:, 0:1], tok_ref[:, 64:65]], axis=0)
    hot16 = (mine == lax.broadcasted_iota(jnp.int32, (16, 512), 1)).astype(F32).astype(BF16)
    hidden0[...] = dot(hot16, emb[...])

    loads[2].wait()
    poles = poles_ref[...][None]
    residues = residues_ref[...][None]
    vocab8 = lax.broadcasted_iota(jnp.int32, (8, 512), 1)

    def filters(g, carry):
        rows = pl.ds(pl.multiple_of(g * 8, 8), 8)
        own_tokens = tokens[n * 8 + g]
        projected = []
        for t in range(STEPS):
            picked = jnp.where(own_tokens[:, t * 64 : t * 64 + 1] == vocab8, scales[0], 0.0)
            scale = jnp.sum(picked, axis=1, keepdims=True)
            projected.append(qkv[pl.ds(pl.multiple_of(t * 64 + g * 8, 8), 8), :] * scale)
        fir0 = [fir_ref[0, c, rows, :] for c in range(3)]
        fir1 = [fir_ref[1, c, rows, :] for c in range(3)]
        proj = [[projected[t][:, c * 256 : (c + 1) * 256] for c in range(3)] for t in range(2)]
        step0 = [
            taps_ref[c : c + 1, :] * proj[0][c]
            + taps_ref[3 + c : 4 + c, :] * fir0[c]
            + taps_ref[6 + c : 7 + c, :] * fir1[c]
            for c in range(3)
        ]
        step1 = [
            taps_ref[c : c + 1, :] * proj[1][c]
            + taps_ref[3 + c : 4 + c, :] * proj[0][c]
            + taps_ref[6 + c : 7 + c, :] * fir0[c]
            for c in range(3)
        ]
        for c in range(3):
            fir_out_ref[0, c, rows, :] = proj[1][c]
            fir_out_ref[1, c, rows, :] = proj[0][c]
        state = modal[rows]
        mixer = []
        for step in (step0, step1):
            gated = step[1] * step[2]
            state = poles * state + gated[:, None, :]
            mixed = jnp.sum(residues * state, axis=1) + skip_ref[...] * gated
            mixer.append(step[0] * mixed)
        modal[rows] = state
        mixers[n, g] = jnp.concatenate(mixer, axis=0).astype(BF16)
        return carry

    def sum_terms(k, carry):
        total = terms[0][k].astype(F32) + terms[1][k].astype(F32) + terms[2][k].astype(F32)
        qkv[pl.ds(pl.multiple_of(k * 16, 16), 16), :] = total
        return carry

    lax.fori_loop(0, 8, sum_terms, 0)
    lax.fori_loop(0, 8, filters, 0)
    modal_store = pltpu.make_async_copy(modal, modal_out_hbm, load_sem.at[7])
    modal_store.start()
    ag_narrow(place, sems, mixers)

    def out_projection(k, rows, weights, sink):
        project_out(rows, weights, [psend.at[k, 0], psend.at[k, 1]])
        gens = []
        for p, axes in enumerate((("y", "x"), ("x", "y"))):
            bufs = (
                r1.at[k, p], t1.at[k, p], m1.at[k, p], r2.at[k, p], t2.at[k, p], l2.at[k, p], r3.at[k, p],
            )
            gens.append(rs_wide_part(place, sems, axes, psend.at[k, p], bufs, sink(p)))
        interleave(*gens)

    loads[3].wait()
    zl, x, y = place.zl, place.x, place.y

    def sink_hidden(p):
        def sink(total):
            cols = pl.ds(p * HALF, HALF)
            hidden1[p] = (hidden0[:, cols] + total).astype(BF16)

        return sink

    out_projection(0, mixers.reshape(512, 256), hyena_out, sink_hidden)
    held[0, y, zl, x] = hidden1[0]
    held[1, x, zl, y] = hidden1[1]
    interleave(
        ag_wide_part(place, sems, ("y", "x"), held.at[0]),
        ag_wide_part(place, sems, ("x", "y"), held.at[1]),
    )

    loads[4].wait()

    def gather_rows(k, carry):
        a = held[0, k // 8, (k // 4) % 2, k % 4]
        b = held[1, k % 4, (k // 4) % 2, k // 8]
        both = jnp.concatenate([a, b], axis=1).astype(F32)
        rows = pl.ds(pl.multiple_of(k * 16, 16), 16)
        emb[rows, :] = (both * both).astype(BF16)
        xg[rows, :] = (both * attn_gain_ref[...]).astype(BF16)
        return carry

    lax.fori_loop(0, 32, gather_rows, 0)
    sums[1] = dot_t(jnp.ones((8, 2048), BF16), emb[...])
    scales_ready = share_scales(place, sems, sums.at[1], sums_got.at[1], scales.at[1])

    for c in range(3):

        def project_qkv(m, carry):
            rows = pl.ds(pl.multiple_of(m * 256, 256), 256)
            got = dot(xg[rows, :], attn_in[c])
            spread[2 * c, rows, :] = got[:, :128]
            spread[2 * c + 1, rows, :] = got[:, 128:]
            return carry

        lax.fori_loop(0, 2, project_qkv, 0)
    for m in range(4):
        for t in range(2):
            for j in range(2):
                for c in range(3):
                    for half in range(2):
                        piece = spread[2 * c + half, pl.ds(t * 8 + m * 2 + j, 32, stride=16), :]
                        first = (t * 2 + j) * 2
                        zsend2 = piece.astype(BF16).reshape(2, 16, 128)
                        att_lanes = slice(c * 256 + half * 128, c * 256 + half * 128 + 128)
                        zsend_b = zsend.at[4 + m]
                        zsend_b[first : first + 2, :, att_lanes] = zsend2
    terms = rs_narrow(place, sems, zsend.at[pl.ds(4, 4)], zcore.at[1], ztemp.at[1], zrecv.at[1])
    scales_ready()

    spread[0:2] = jnp.zeros((2, 512, 128), F32)
    for tj in range(4):
        t, j = tj // 2, tj % 2
        lane = lax.broadcasted_iota(jnp.int32, (32, 512), 1)
        row = lax.broadcasted_iota(jnp.int32, (32, 512), 0)
        wanted = row * 16 + t * 8 + n * 2 + j
        scale = jnp.sum(jnp.where(lane == wanted, scales[1][0:1, :], 0.0), axis=1, keepdims=True)
        rows = slice(tj * 2, tj * 2 + 2)
        total = (
            terms[0][rows].astype(F32) + terms[1][rows].astype(F32) + terms[2][rows].astype(F32)
        ).reshape(32, 768) * scale
        for c in range(3):
            at = j * 8 + (t if c == 0 else 4 + 2 * t + (c - 1))
            for half in range(2):
                lo = c * 256 + half * 128
                spread[half, pl.ds(at, 32, stride=16), :] = total[:, lo : lo + 128]

    def pack(k, carry):
        rows = pl.ds(pl.multiple_of(k * 16, 16), 16)
        both = jnp.concatenate([spread[0, rows, :], spread[1, rows, :]], axis=1)
        spread16[k] = both.astype(BF16)
        return carry

    lax.fori_loop(0, 32, pack, 0)
    routed_ready = all_to_all(place, sems, spread16, routed)
    pltpu.make_async_copy(kv_raw, kv_raw, load_sem.at[6]).wait()
    kv = kv_raw.reshape(2, 64, 128, 128)
    routed_ready()

    cos, sin = cos_ref[...], sin_ref[...]
    lane = lax.broadcasted_iota(jnp.int32, (16, 128), 1)
    row = lax.broadcasted_iota(jnp.int32, (16, 128), 0)
    position = lane // 2
    valid = (lane % 2 == 0) & (
        (position < len_ref[...])
        | (position == 62)
        | ((position == 63) & (row % 8 == 1))
    )
    top_rows = lax.broadcasted_iota(jnp.int32, (8, 128), 0)
    inv = 1.0 / math.sqrt(HEAD_DIM)

    def attend(k, carry):
        message = jnp.zeros((8, 128), F32)
        for hh in range(2):
            h = k * 2 + hh
            vectors = routed[k, :, hh * 128 : hh * 128 + 128].astype(F32)
            turned = vectors * cos + pltpu.roll(vectors, 64, axis=1) * sin
            turned16 = turned.astype(BF16)
            scores = []
            for j in range(2):
                old = kv[j, h, 112:128, :].astype(F32)
                fresh = jnp.where(top_rows >= 4, turned[j * 8 : j * 8 + 8], old[8:16])
                kv[j, h, 112:128, :] = jnp.concatenate([old[0:8], fresh], axis=0).astype(BF16)
                scores.append(dot_t(turned16, kv[j, h])[j * 8 : j * 8 + 8])
            score = jnp.where(valid, jnp.concatenate(scores, axis=0) * inv, -1e30)
            grown = jnp.exp(score - jnp.max(score, axis=1, keepdims=True))
            weight = grown / jnp.sum(grown, axis=1, keepdims=True)
            weight16 = pltpu.roll(weight, 1, axis=1).astype(BF16)
            for j in range(2):
                got = dot(weight16, kv[j, h])[j * 8 : j * 8 + 8]
                at = hh * 4 + j * 2
                moved = pltpu.roll(got, at, axis=0) if at else got
                message = jnp.where((top_rows >= at) & (top_rows < at + 2), moved, message)
        att_send[k] = message.astype(BF16).astype(F32)
        return carry

    lax.fori_loop(0, 32, attend, 0)
    all_to_all(place, sems, att_send, att_recv)()
    flat = att_recv.reshape(256, 128)
    for jt in range(4):
        for hh in range(2):
            piece = flat[pl.ds(hh * 4 + jt, 32, stride=8), :]
            att_rows[n, jt * 2 : jt * 2 + 2, :, hh * 128 : hh * 128 + 128] = piece.astype(BF16).reshape(
                2, 16, 128
            )
    ag_narrow(place, sems, att_rows)
    for m in range(4):
        for jt in range(4):
            j, t = jt // 2, jt % 2
            for hh in range(2):
                piece = att_rows[m, jt * 2 : jt * 2 + 2, :, hh * 128 : hh * 128 + 128].astype(F32)
                spread[hh, pl.ds(t * 8 + m * 2 + j, 32, stride=16), :] = piece.reshape(32, 128)

    def pack_rows(k, carry):
        rows = pl.ds(pl.multiple_of(k * 64, 64), 64)
        both = jnp.concatenate([spread[0, rows, :], spread[1, rows, :]], axis=1)
        att_full[rows, :] = both.astype(BF16)
        return carry

    lax.fori_loop(0, 8, pack_rows, 0)
    loads[5].wait()

    def sink_out(p):
        def sink(total):
            cols = pl.ds(p * HALF, HALF)
            out_ref[:, cols] = (hidden1[p].astype(F32) + total).astype(BF16)

        return sink

    out_projection(1, att_full, attn_out, sink_out)
    modal_store.wait()


def local(
    token_ids,
    lengths,
    embedding,
    hyena_gain,
    hyena_in,
    fir_taps,
    poles,
    residues,
    skip,
    hyena_out,
    modal_state,
    fir_state,
    attn_gain,
    attn_in,
    attn_out,
    kv_cache,
):
    tok = jnp.repeat(token_ids.T, 64, axis=1)
    half = HEAD_DIM // 2
    freqs = jnp.exp(-math.log(10000.0) * jnp.arange(half, dtype=F32) * 2.0 / HEAD_DIM)
    step = jnp.array([0, 1, 0, 0, 0, 0, 1, 0], jnp.int32)
    turns = jnp.array([1, 1, 0, 0, 1, 0, 1, 0], F32)
    angles = ((lengths[:, None] + step[None, :]).astype(F32) * turns[None, :])[..., None] * freqs
    cosine = jnp.cos(angles).reshape(16, half)
    sine = jnp.sin(angles).reshape(16, half)
    cos = jnp.concatenate([cosine, cosine], axis=1)
    sin = jnp.concatenate([-sine, sine], axis=1)
    lens = jnp.broadcast_to(lengths[:, None, None], (2, 8, 128)).reshape(16, 128)
    vmem = pl.BlockSpec(memory_space=pltpu.VMEM)
    anywhere = pl.BlockSpec(memory_space=pl.ANY)

    out, modal_out, fir_out = pl.pallas_call(
        kernel,
        out_shape=(
            jax.ShapeDtypeStruct((16, 2048), BF16),
            jax.ShapeDtypeStruct((64, 16, 256), F32),
            jax.ShapeDtypeStruct((2, 3, 64, 256), F32),
        ),
        in_specs=[vmem] * 11 + [anywhere] * 7,
        out_specs=(vmem, anywhere, vmem),
        scratch_shapes=[
            pltpu.VMEM((512, 2048), BF16),
            pltpu.VMEM((3, 2048, 256), BF16),
            pltpu.VMEM((64, 16, 256), F32),
            pltpu.VMEM((256, 2048), BF16),
            pltpu.VMEM((3, 2048, 256), BF16),
            pltpu.VMEM((256, 2048), BF16),
            pltpu.VMEM((2, 64, 64, 2, 128), BF16),
            pltpu.SemaphoreType.DMA((8,)),
            pltpu.SemaphoreType.DMA((256,)),
            pltpu.SemaphoreType.DMA((256,)),
            pltpu.VMEM((32, 8, 128), jnp.int32),
            pltpu.VMEM((512, 2048), BF16),
            pltpu.VMEM((3, 512, 256), BF16),
            pltpu.VMEM((8, 8, 16, 768), BF16),
            pltpu.VMEM((2, 2, 8, 16, 768), BF16),
            pltpu.VMEM((2, 8, 16, 768), BF16),
            pltpu.VMEM((2, 8, 16, 768), BF16),
            pltpu.VMEM((2, 8, 512), F32),
            pltpu.VMEM((2, 3, 8, 512), F32),
            pltpu.VMEM((2, 8, 512), F32),
            pltpu.VMEM((4, 8, 16, 256), BF16),
            pltpu.VMEM((2, 2, 4, 2, 4, 16, HALF), BF16),
            pltpu.VMEM((2, 2, 2, 3, 4, 16, HALF), BF16),
            pltpu.VMEM((2, 2, 2, 4, 16, HALF), BF16),
            pltpu.VMEM((2, 2, 4, 2, 1, 16, HALF), BF16),
            pltpu.VMEM((2, 2, 2, 3, 1, 16, HALF), BF16),
            pltpu.VMEM((2, 2, 2, 1, 16, HALF), BF16),
            pltpu.VMEM((2, 2, 2, 16, HALF), BF16),
            pltpu.VMEM((2, 2, 16, HALF), BF16),
            pltpu.VMEM((16, 2048), F32),
            pltpu.VMEM((2, 16, HALF), BF16),
            pltpu.VMEM((2, 4, 2, 4, 16, HALF), BF16),
            pltpu.VMEM((128, 768), F32),
            pltpu.VMEM((6, 512, 128), F32),
            pltpu.VMEM((32, 16, 256), BF16),
            pltpu.VMEM((32, 16, 256), BF16),
            pltpu.VMEM((32, 8, 128), F32),
            pltpu.VMEM((32, 8, 128), F32),
            pltpu.VMEM((4, 8, 16, 256), BF16),
            pltpu.VMEM((512, 256), BF16),
        ],
        compiler_params=pltpu.CompilerParams(
            collective_id=0, has_side_effects=True, vmem_limit_bytes=56 * 1024 * 1024
        ),
        name="decode",
    )(
        tok,
        hyena_gain[None, :],
        attn_gain[None, :],
        fir_taps.reshape(9, 256),
        poles,
        residues,
        skip[None, :],
        fir_state.transpose(1, 2, 0, 3),
        cos,
        sin,
        lens,
        embedding,
        hyena_in.transpose(1, 0, 2),
        modal_state,
        hyena_out,
        attn_in.transpose(1, 0, 2),
        attn_out,
        kv_cache,
    )
    return out.reshape(2, 8, 2048), modal_out, fir_out.transpose(2, 0, 1, 3)


def solution(mesh):
    placed = (
        P(None, "wide"),
        P(("wide", "narrow")),
        P(None, "narrow"),
        P("narrow"),
        P("narrow", None, "wide"),
        P(None, None, "wide"),
        P(None, "wide"),
        P(None, "wide"),
        P("wide"),
        P("wide", "narrow"),
        P("narrow", None, "wide"),
        P("narrow", None, None, "wide"),
        P("narrow"),
        P("narrow", None, "wide"),
        P("wide", "narrow"),
        P(("wide", "narrow"), None, None, None),
    )
    return jax.shard_map(
        local,
        mesh=mesh,
        in_specs=placed,
        out_specs=(
            P(None, "wide", "narrow"),
            P("narrow", None, "wide"),
            P("narrow", None, None, "wide"),
        ),
        check_vma=False,
    )
```

time: 1460 us -> 177 us (0.12)
  waiting for transfers between devices: 1270 us -> 0 us
  Pallas kernels: 0 us -> 162 us
  blocking collectives: 69.2 us -> 0 us
  matrix products: 30.6 us -> 0 us
  local copies, waits for them, and re-layouts: 43.1 us -> 13.3 us
  starting transfers between devices: 15.1 us -> 0 us
    reduce_scatter x8 -> x0, waiting for transfers between devices: 680 us -> none  [the longest x2 310 us: local(): lax.psum_scatter(jnp.dot(mixer_all, hyena_out, preferred_element_type=jnp...]
    all_gather x4 -> x0, waiting for transfers between devices: 583 us -> none  [the longest x2 294 us: local(): lax.all_gather(normed0, 'wide', axis=0, tiled=True)]
    pallas_call x0 -> x1, Pallas kernels: none -> 162 us  [local(): pl.pallas_call(kernel, out_shape=(jax.ShapeDtypeStruct((16, 2048), BF16),...]
    dot_general x16 -> x0, matrix products: 30.6 us -> none  [the longest x2 8.28 us: local(): jnp.dot(lax.all_gather(normed1, 'wide', axis=0, tiled=True), qkv_matrix,...]
    all_gather x4 -> x0, blocking collectives: 27.7 us -> none  [the longest x2 13.9 us: local(): mixer_all = lax.all_gather(mixer, 'narrow', axis=0, tiled=True)]
    all_to_all x2 -> x0, blocking collectives: 23.5 us -> none  [local(): lax.all_to_all(pieces, 'wide', split_axis=1, concat_axis=0, tiled=True)]
    slice x2 -> x0, local copies, waits for them, and re-layouts: 22.9 us -> none  [the longest x1 21.9 us: attend_local(): keys = cache[:, :, 0].reshape(rows, span, HEADS, HEAD_DIM)]
    psum x2 -> x0, blocking collectives: 18 us -> none  [norm_rows(): total = lax.psum(jnp.sum(values * values, axis=1), 'narrow')]
  transfers between devices with their start and end apart: 14 -> 0, of which waited for: 13 -> 0; matrix products, arithmetic and copies ran while one was open for 5% -> 0% of each run, Pallas kernels for 0% -> 0%
where the time goes in v1:
time: 177 us
  Pallas kernels  162 us (92%)
  local copies, waits for them, and re-layouts  13.3 us (8%)
    pallas_call x1, Pallas kernels, local(): pl.pallas_call(kernel, out_shape=(jax.ShapeDtypeStruct((16, 2048), BF16),...  162 us
    unnamed x4, local copies, waits for them, and re-layouts  7.56 us

profile of v1, /device:TPU:0, one launch (start us, length us, event | category | flops | bytes accessed | tf_op | source)
XLA Modules:
  0.0 176.7 jit_solution(17999240432054246127)
XLA Ops:
  0.6 0.7 add.23
  1.3 0.1 add.24
  1.4 0.7 mul.34
  2.0 0.1 mul.35
  2.1 0.7 add.21
  2.9 0.1 add.22
  2.9 0.8 copy.21
  3.7 0.1 broadcast_in_dim.10
  3.8 0.7 reshape.64.tok_ref
  4.5 0.7 broadcast_in_dim.27.len_ref
  5.1 1.3 reshape.65.taps_ref
  6.4 0.1 fusion
  6.6 0.7 pad_maximum_fusion
  7.2 1.8 %copy.25 = f32[64,2,3,256]{3,0,2,1:T(8,128)} copy(f32[64,2,3,256]{3,1,2,0:T(2,128)} %param.29) | data formatting | bytes 786432 | tf_op args[11]
  9.0 161.9 %decode.1 = (bf16[16,2048]{1,0:T(8,128)(2,1)}, f32[64,16,256]{2,1,0:T(8,128)}, f32[2,3,64,256]{3,2,1,0:T(8,128)}) custom-call(s32[8,128]{1,0:T(8,128)} %reshape.64.tok_ref, f32[1,2048]{1,0:T(1,128)} %bitcast.20, f32[1,2048]{1,0:T(1,128)} %bitcast.21, f32[9,256]{1,0:T(8,128)} %reshape.65.taps_ref, f32[16,256]{1,0:T(8,128)} %poles_ref.1, ...), custom_call_target="tpu_custom_call" | custom-call | tf_op jit(solution)/shard_map/decode/pallas_call | solution.py:721
  170.9 2.0 %copy.23 = f32[64,2,3,256]{3,1,2,0:T(2,128)} copy(f32[64,2,3,256]{3,0,2,1:T(8,128)} %bitcast.18) | data formatting | bytes 786432
  172.9 1.5 copy.28
  174.4 2.3 %copy.29 = f32[64,16,256]{2,1,0:T(8,128)} copy(f32[64,16,256]{2,1,0:T(8,128)} %get-tuple-element.21) | data formatting | bytes 2097152
  (2 shorter events, 0.0 us)

commit v2 on v0

v2 whole, which is shorter than its diff:
```python
import math

import jax
import jax.numpy as jnp
from jax import lax
from jax.experimental import pallas as pl
from jax.experimental.pallas import tpu as pltpu
from jax.sharding import PartitionSpec as P

D = 8192
HEADS = 64
HEAD_DIM = 128
STEPS = 2
EPS = 1e-06
MESH = pl.DeviceIdType.MESH
F32 = jnp.float32
BF16 = jnp.bfloat16
HALF = 1024


def dot(a, b):
    return jnp.dot(a, b, preferred_element_type=F32)


def dot_t(a, b):
    return lax.dot_general(a, b, (((1,), (1,)), ((), ())), preferred_element_type=F32)


class Place:
    def __init__(self):
        self.w = lax.axis_index("wide")
        self.n = lax.axis_index("narrow")
        self.y = self.w // 8
        self.zl = (self.w // 4) % 2
        self.x = self.w % 4
        self.zh = self.n // 2
        self.c = self.n % 2

    def along(self, axis, step):
        y = (self.y + step) % 4 if axis == "y" else self.y
        x = (self.x + step) % 4 if axis == "x" else self.x
        zl = (self.zl + step) % 2 if axis == "zl" else self.zl
        return ((y * 2 + zl) * 4 + x, self.n)

    def shifted(self, axis, step, dzl):
        y = (self.y + step) % 4 if axis == "y" else self.y
        x = (self.x + step) % 4 if axis == "x" else self.x
        return ((y * 2 + (self.zl + dzl) % 2) * 4 + x, self.n)

    def narrow(self, dzh, dc):
        return (self.w, ((self.zh + dzh) % 2) * 2 + (self.c + dc) % 2)


class Sems:
    def __init__(self, send, recv):
        self.send, self.recv, self.sends, self.recvs = send, recv, 0, 0

    def sender(self):
        self.sends += 1
        return self.send.at[self.sends - 1]

    def receiver(self):
        self.recvs += 1
        return self.recv.at[self.recvs - 1]


def push(src, dst, send_sem, recv_sem, device):
    pltpu.make_async_remote_copy(
        src_ref=src,
        dst_ref=dst,
        send_sem=send_sem,
        recv_sem=recv_sem,
        device_id=device,
        device_id_type=MESH,
    ).start()


def drain(sem, like):
    pltpu.make_async_copy(like, like, sem).wait()


def total_of(*terms):
    total = terms[0].astype(F32)
    for term in terms[1:]:
        total = total + term.astype(F32)
    return total


def rs_wide_part(place, sems, axes, src, bufs, fill, out):
    far, close, temp, mid, inbox = bufs
    send_sem, far_sem, close_sem, in_sem = sems
    first, second = axes
    f, s = getattr(place, first), getattr(place, second)
    zs = (place.zl, 1 - place.zl)
    steps = (1, 3)

    def block(step, h, o):
        return ((f + step) % 4) * 8 + zs[h] * 4 + (s + o) % 4

    def hand_on(o):
        drain(far_sem.at[o], far.at[o])
        for h in (1, 0):
            temp[o, h] = total_of(src[block(steps[h], h, o)], far[o, h]).astype(BF16)
            push(temp.at[o, h], close.at[o, h], send_sem, close_sem.at[o], place.along(first, steps[h]))

    def send_close(o):
        for h in (1, 0):
            step = steps[1 - h]
            push(src.at[block(step, h, o)], close.at[o, 2 + h], send_sem, close_sem.at[o], place.along(first, step))

    def finish(o):
        drain(close_sem.at[o], close.at[o])
        for h in (1, 0):
            total = total_of(src[block(0, h, o)], close[o, h], close[o, 2 + h])
            if h or o:
                mid[h * 4 + o] = total.astype(BF16)
                there = place.shifted(second, o, h)
                push(mid.at[h * 4 + o], inbox.at[h * 4 + o], send_sem, in_sem, there)
        return total

    fill((f + 2) % 4)
    for o in (2, 1, 3, 0):
        for h in (1, 0):
            push(src.at[block(2, h, o)], far.at[o, h], send_sem, far_sem.at[o], place.along(first, steps[h]))
    yield
    fill((f + 1) % 4)
    fill((f + 3) % 4)
    send_close(2)
    yield
    hand_on(2)
    send_close(1)
    send_close(3)
    yield
    fill(f)
    hand_on(1)
    hand_on(3)
    send_close(0)
    yield
    hand_on(0)
    yield
    finish(2)
    yield
    finish(1)
    finish(3)
    yield
    total = finish(0)
    yield
    drain(in_sem, inbox.at[pl.ds(1, 7)])
    for k in range(1, 8):
        total = total + inbox[k].astype(F32)
    out(total)
    drain(send_sem, src.at[pl.ds(0, 31)])


def ag_wide_part(place, sems, axes, held):
    first, second = axes
    f, s = getattr(place, first), getattr(place, second)
    zs = (place.zl, 1 - place.zl)
    steps = (1, 3)
    send_sem, in_sem, pass_sem, end_sem = sems

    def block(step, h, o):
        return held.at[((f + step) % 4) * 8 + zs[h] * 4 + (s + o) % 4]

    def ring(h, o):
        for d, step in enumerate(steps):
            sem = pass_sem.at[h * 4 + o] if d == h else end_sem
            push(block(0, h, o), block(0, h, o), send_sem, sem, place.along(first, step))

    def arrive(h, o):
        drain(in_sem.at[h * 4 + o], block(0, h, o))
        ring(h, o)

    def pass_on(h, o):
        drain(pass_sem.at[h * 4 + o], block(0, h, o))
        got = block(4 - steps[h], h, o)
        push(got, got, send_sem, end_sem, place.along(first, steps[h]))

    own = block(0, 0, 0)
    order = ((1, 0), (0, 1), (0, 3), (1, 1), (1, 3), (0, 2), (1, 2))
    for h, o in order:
        push(own, own, send_sem, in_sem.at[h * 4 + (4 - o) % 4], place.shifted(second, o, h))
        if (h, o) == (0, 3):
            ring(0, 0)
    yield
    arrive(1, 0)
    yield
    arrive(0, 1)
    arrive(0, 3)
    yield
    pass_on(0, 0)
    yield
    arrive(1, 1)
    arrive(1, 3)
    yield
    pass_on(1, 0)
    yield
    arrive(0, 2)
    arrive(1, 2)
    yield
    for h, o in ((0, 1), (0, 3), (1, 1), (1, 3)):
        pass_on(h, o)
    yield
    for h, o in ((0, 2), (1, 2)):
        pass_on(h, o)
    yield
    drain(end_sem, held.at[pl.ds(0, 16)])
    drain(send_sem, held.at[pl.ds(0, 31)])


def interleave(*parts):
    parts = list(parts)
    while parts:
        left = []
        for part in parts:
            try:
                next(part)
                left.append(part)
            except StopIteration:
                pass
        parts = left


def rs_narrow(place, sems, src, fill, core_recv, temp, z_recv):
    zh, c = place.zh, place.c
    mate, across = place.narrow(0, 1), place.narrow(1, 0)
    parts = [pl.ds(p * 4, 4) for p in range(2)]
    send_sem, near_sem = sems.sender(), sems.receiver()
    far_sems = [sems.receiver() for p in parts]
    cross_sems = [sems.receiver() for p in parts]
    over = (1 - zh) * 2 + 1 - c
    fill(over)
    for p, far_sem in zip(parts, far_sems):
        push(src.at[over, p], core_recv.at[0, p], send_sem, far_sem, mate)
    over = (1 - zh) * 2 + c
    fill(over)
    for p, far_sem, cross_sem in zip(parts, far_sems, cross_sems):
        drain(far_sem, temp.at[p])
        temp[p] = total_of(src[over, p], core_recv[0, p]).astype(BF16)
        push(temp.at[p], z_recv.at[p], send_sem, cross_sem, across)
    fill(zh * 2 + 1 - c)
    push(src.at[zh * 2 + 1 - c], core_recv.at[1], send_sem, near_sem, mate)
    fill(zh * 2 + c)
    drain(near_sem, z_recv)
    for p, cross_sem in zip(parts, cross_sems):
        drain(cross_sem, z_recv.at[p])
    drain(send_sem, src.at[pl.ds(0, 3)])
    return [src.at[zh * 2 + c], core_recv.at[1], z_recv]


def ag_narrow(place, sems, held):
    zh, c = place.zh, place.c
    own = held.at[place.n]
    send_sem, cross_sem, core_sem = sems.sender(), sems.receiver(), sems.receiver()
    push(own, own, send_sem, cross_sem, place.narrow(1, 0))
    push(own, own, send_sem, core_sem, place.narrow(0, 1))
    drain(cross_sem, own)
    got = held.at[(1 - zh) * 2 + c]
    push(got, got, send_sem, core_sem, place.narrow(0, 1))
    drain(core_sem, held.at[pl.ds(0, 2)])
    drain(send_sem, held.at[pl.ds(0, 3)])


def share_scales(place, sems, sums, got, scales):
    send_sem, recv_sem = sems.sender(), sems.receiver()
    for k, (dzh, dc) in enumerate(((0, 1), (1, 0), (1, 1))):
        push(sums, got.at[k], send_sem, recv_sem, place.narrow(dzh, dc))

    def finish():
        drain(recv_sem, got)
        drain(send_sem, got)
        total = sums[...] + got[0] + got[1] + got[2]
        scales[...] = lax.rsqrt(total / D + EPS)

    return finish


def kernel(
    tok_ref,
    len_ref,
    hyena_gain_ref,
    attn_gain_ref,
    taps_ref,
    poles_ref,
    residues_ref,
    skip_ref,
    fir_hbm,
    emb_hbm,
    hyena_in_hbm,
    modal_hbm,
    hyena_out_hbm,
    attn_in_hbm,
    attn_out_hbm,
    kv_hbm,
    out_ref,
    modal_out_hbm,
    fir_out_hbm,
    emb,
    hyena_in,
    modal,
    hyena_out,
    attn_in,
    attn_out,
    kv_raw,
    fir_raw,
    load_sem,
    send_sem,
    recv_sem,
    rs_sem,
    ag_sem,
    tokens,
    xg,
    table,
    zsend,
    zcore,
    ztemp,
    zrecv,
    sums,
    sums_got,
    scales,
    mixers,
    psend,
    far,
    close,
    temp,
    mid,
    inbox,
    hidden0,
    hidden1,
    held,
    qkv,
    wide_qkv,
    spread,
    spread16,
    routed,
    turned16,
    scored,
    weights16,
    att_send,
    att_recv,
    att_rows,
    att_full,
):
    place = Place()
    sems = Sems(send_sem, recv_sem)
    w, n = place.w, place.n

    barrier = pltpu.get_barrier_semaphore()

    def peer(d):
        return ((w + d) % 32, ((place.zh + d // 32) % 2) * 2 + place.c)

    def greet(d, carry):
        pl.semaphore_signal(barrier, inc=1, device_id=peer(d), device_id_type=MESH)
        return carry

    lax.fori_loop(1, 64, greet, 0)
    for dzh in range(2):
        pl.semaphore_signal(barrier, inc=1, device_id=place.narrow(dzh, 1), device_id_type=MESH)

    loads = []
    for k, (src, dst) in enumerate(
        (
            (emb_hbm, emb),
            (hyena_in_hbm, hyena_in),
            (modal_hbm, modal),
            (hyena_out_hbm, hyena_out),
            (attn_in_hbm, attn_in),
            (attn_out_hbm, attn_out),
        )
    ):
        copy = pltpu.make_async_copy(src, dst, load_sem.at[k])
        loads.append(copy)
    loads[0].start()
    loads[1].start()
    loads[2].start()
    fir = fir_raw.reshape(6, 128, 128)
    for c in range(3):
        for half in range(2):
            pltpu.make_async_copy(
                fir_hbm.at[:, c, :, pl.ds(half * 128, 128)], fir_raw.at[c * 2 + half], load_sem.at[8]
            ).start()
    loads[3].start()

    sub8 = lax.broadcasted_iota(jnp.int32, (8, 128), 0)
    lane8 = lax.broadcasted_iota(jnp.int32, (8, 128), 1)
    tile = jnp.zeros((8, 128), jnp.int32)
    for t in range(STEPS):
        for i in range(8):
            tile = jnp.where((sub8 == i) & (lane8 // 64 == t), tok_ref[t, i], tile)
    tokens[w] = tile
    token_send, token_recv = sems.sender(), sems.receiver()

    def token_start(d, carry):
        push(tokens.at[w], tokens.at[w], token_send, token_recv, peer(d))
        return carry

    pl.semaphore_wait(barrier, 65)
    lax.fori_loop(1, 32, token_start, 0)

    lane16 = lax.broadcasted_iota(jnp.int32, (16, 128), 1)
    sub16 = lax.broadcasted_iota(jnp.int32, (16, 128), 0)
    loads[0].wait()

    def gain_rows(k, squares):
        rows = pl.ds(pl.multiple_of(k * 16, 16), 16)
        values = emb[rows, :].astype(F32)
        xg[rows, :] = (values * hyena_gain_ref[...]).astype(BF16)
        return jnp.where(lane16 == k, jnp.sum(values * values, axis=1, keepdims=True), squares)

    sums[0] = lax.fori_loop(0, 32, gain_rows, jnp.zeros((16, 128), F32), unroll=4)
    scales_ready = share_scales(place, sems, sums.at[0], sums_got.at[0], scales.at[0])

    def load_kv(h, carry):
        for j in range(2):
            lanes = pl.ds(pl.multiple_of(h * 128, 128), 128)
            pltpu.make_async_copy(kv_hbm.at[j, :, :, lanes], kv_raw.at[h, j], load_sem.at[6]).start()
        return carry

    loads[1].wait()

    def project(k, carry):
        c, m = k // 2, k % 2
        rows = pl.ds(pl.multiple_of(m * 256, 256), 256)
        table[c, rows, :] = dot(xg[rows, :], hyena_in[c]).astype(BF16)
        return carry

    lax.fori_loop(0, 6, project, 0)
    loads[4].start()
    loads[5].start()
    lax.fori_loop(0, 64, load_kv, 0)

    drain(token_recv, tokens.at[pl.ds(0, 31)])
    drain(token_send, tokens.at[pl.ds(0, 31)])
    vocab = lax.broadcasted_iota(jnp.int32, (64, 512), 1)

    def pick(m):
        rows = tokens[pl.ds(m * 8, 8)].reshape(64, 128)
        for t in range(STEPS):
            hot = (rows[:, t * 64 : t * 64 + 1] == vocab).astype(F32).astype(BF16)
            for c in range(3):
                picked = dot(hot, table[c]).astype(BF16).reshape(4, 16, 256)
                zsend[0, m, t * 4 : t * 4 + 4, :, c * 256 : (c + 1) * 256] = picked

    terms = rs_narrow(place, sems, zsend.at[0], pick, zcore.at[0], ztemp.at[0], zrecv.at[0])
    scales_ready()

    own = tokens[w]
    mine = jnp.concatenate([own[:, 0:1], own[:, 64:65]], axis=0)
    hot16 = (mine == lax.broadcasted_iota(jnp.int32, (16, 512), 1)).astype(F32).astype(BF16)
    hidden0[...] = dot(hot16, emb[...])

    loads[2].wait()
    pltpu.make_async_copy(fir_raw, fir_raw, load_sem.at[8]).wait()
    poles = poles_ref[...][None]
    residues = residues_ref[...][None]

    def filters(g, carry):
        rows = pl.ds(pl.multiple_of(g * 8, 8), 8)
        own_tokens = tokens[n * 8 + g]
        proj = []
        for t in range(STEPS):
            column = own_tokens[:, t * 64 : t * 64 + 1]
            picked = jnp.zeros((8, 128), F32)
            for r in range(16):
                picked = jnp.where(column == lane8 * 16 + r, scales[0, r : r + 1, :], picked)
            scale = jnp.sum(picked, axis=1, keepdims=True)
            got = qkv[pl.ds(pl.multiple_of(t * 64 + g * 8, 8), 8), :] * scale
            proj.append([got[:, c * 256 : (c + 1) * 256] for c in range(3)])
        olds = []
        for slot in range(2):
            old = []
            for c in range(3):
                halves = [fir[c * 2 + half, pl.ds(g * 16 + slot, 8, stride=2), :] for half in range(2)]
                old.append(jnp.concatenate(halves, axis=1))
            olds.append(old)
        taps = [[taps_ref[k, c : c + 1, :] for c in range(3)] for k in range(3)]
        step0 = [taps[0][c] * proj[0][c] + taps[1][c] * olds[0][c] + taps[2][c] * olds[1][c] for c in range(3)]
        step1 = [taps[0][c] * proj[1][c] + taps[1][c] * proj[0][c] + taps[2][c] * olds[0][c] for c in range(3)]
        for slot in range(2):
            for c in range(3):
                for half in range(2):
                    fir[c * 2 + half, pl.ds(g * 16 + slot, 8, stride=2), :] = proj[1 - slot][c][
                        :, half * 128 : half * 128 + 128
                    ]
        state = modal[rows]
        mixer = []
        for step in (step0, step1):
            gated = step[1] * step[2]
            state = poles * state + gated[:, None, :]
            mixed = jnp.sum(residues * state, axis=1) + skip_ref[...] * gated
            mixer.append(step[0] * mixed)
        modal[rows] = state
        mixers[n, g] = jnp.concatenate(mixer, axis=0).astype(BF16)
        return carry

    def sum_terms(k, carry):
        qkv[pl.ds(pl.multiple_of(k * 16, 16), 16), :] = total_of(terms[0][k], terms[1][k], terms[2][k])
        return carry

    lax.fori_loop(0, 8, sum_terms, 0)
    lax.fori_loop(0, 8, filters, 0)
    modal_store = pltpu.make_async_copy(modal, modal_out_hbm, load_sem.at[7])
    modal_store.start()
    for c in range(3):
        for half in range(2):
            pltpu.make_async_copy(
                fir_raw.at[c * 2 + half], fir_out_hbm.at[:, c, :, pl.ds(half * 128, 128)], load_sem.at[8]
            ).start()
    ag_narrow(place, sems, mixers)

    def out_projection(k, rows, weights, sink):
        def fill_a(y):
            block = rows[pl.ds(y * 8, 8)].reshape(128, 256)
            psend[k, 0, pl.ds(y * 8, 8)] = dot(block, weights[:, :HALF]).astype(BF16).reshape(8, 16, HALF)

        def fill_b(x):
            block = jnp.concatenate(
                [rows[(y * 2 + zl) * 4 + x] for zl in range(2) for y in range(4)], axis=0
            )
            psend[k, 1, pl.ds(x * 8, 8)] = dot(block, weights[:, HALF:]).astype(BF16).reshape(8, 16, HALF)

        gens = []
        for p, (axes, fill) in enumerate(((("y", "x"), fill_a), (("x", "y"), fill_b))):
            bufs = [b.at[k, p] for b in (far, close, temp, mid, inbox)]
            sem = rs_sem.at[k, p]
            rs_sems = (sems.sender(), sem.at[pl.ds(0, 4)], sem.at[pl.ds(4, 4)], sem.at[8])
            gens.append(rs_wide_part(place, rs_sems, axes, psend.at[k, p], bufs, fill, sink(p)))
        interleave(*gens)

    loads[3].wait()
    zl, x, y = place.zl, place.x, place.y

    def sink_hidden(p):
        def sink(total):
            cols = pl.ds(p * HALF, HALF)
            hidden1[p] = (hidden0[:, cols] + total).astype(BF16)

        return sink

    out_projection(0, mixers.reshape(32, 16, 256), hyena_out, sink_hidden)
    held[0, (y * 2 + zl) * 4 + x] = hidden1[0]
    held[1, (x * 2 + zl) * 4 + y] = hidden1[1]
    squares = jnp.sum(total_of(hidden1[0]) ** 2 + total_of(hidden1[1]) ** 2, axis=1, keepdims=True)
    sums[1] = jnp.broadcast_to(squares, (16, 128))
    scales_ready = share_scales(place, sems, sums.at[1], sums_got.at[1], scales.at[1])
    gens = []
    for p, axes in enumerate((("y", "x"), ("x", "y"))):
        sem = ag_sem.at[p]
        ag_sems = (sems.sender(), sem.at[pl.ds(0, 8)], sem.at[pl.ds(8, 8)], sem.at[16])
        gens.append(ag_wide_part(place, ag_sems, axes, held.at[p]))
    interleave(*gens)

    loads[4].wait()

    def gather_rows(k, carry):
        a = held[0, k]
        b = held[1, ((k % 4) * 2 + (k // 4) % 2) * 4 + k // 8]
        both = jnp.concatenate([a, b], axis=1).astype(F32)
        rows = pl.ds(pl.multiple_of(k * 16, 16), 16)
        xg[rows, :] = (both * attn_gain_ref[...]).astype(BF16)
        return carry

    lax.fori_loop(0, 32, gather_rows, 0, unroll=4)

    for c in range(3):

        def project_qkv(m, carry):
            rows = pl.ds(pl.multiple_of(m * 256, 256), 256)
            got = dot(xg[rows, :], attn_in[c])
            wide_qkv[2 * c, rows, :] = got[:, :128]
            wide_qkv[2 * c + 1, rows, :] = got[:, 128:]
            return carry

        lax.fori_loop(0, 2, project_qkv, 0)

    def split(m):
        for t in range(2):
            for j in range(2):
                first = (t * 2 + j) * 2
                for c in range(3):
                    for half in range(2):
                        piece = wide_qkv[2 * c + half, pl.ds(t * 8 + m * 2 + j, 32, stride=16), :]
                        lanes = slice(c * 256 + half * 128, c * 256 + half * 128 + 128)
                        zsend[1, m, first : first + 2, :, lanes] = piece.astype(BF16).reshape(2, 16, 128)

    zh, core = place.zh, place.c
    mate = place.narrow(0, 1)
    core_send = sems.sender()
    core_recv = [sems.receiver(), sems.receiver()]
    route_send, route_recv = sems.sender(), sems.receiver()
    for d in (1, 0):
        half = (zh + d) % 2
        split(half * 2 + 1 - core)
        push(zsend.at[1, half * 2 + 1 - core], zcore.at[1, half], core_send, core_recv[d], mate)
    for half in range(2):
        spread[half] = jnp.zeros((512, 128), F32)
        spread[2 + half] = jnp.zeros((512, 128), F32)
    for d in (1, 0):
        across = (zh + d) % 2
        for tj in range(4):
            t, j = tj // 2, tj % 2
            if tj == 0:
                split(across * 2 + core)
                drain(core_recv[d], zcore.at[1, 0])
            rows = slice(tj * 2, tj * 2 + 2)
            total = total_of(zsend[1, across * 2 + core, rows], zcore[1, across, rows]).reshape(32, 768)
            for c in range(3):
                at = j * 8 + (t if c == 0 else 4 + 2 * t + (c - 1))
                for half in range(2):
                    lo = c * 256 + half * 128
                    spread[2 * d + half, pl.ds(at, 32, stride=16), :] = total[:, lo : lo + 128]

        def pack(k, carry):
            rows = pl.ds(pl.multiple_of(k * 16, 16), 16)
            both = jnp.concatenate([spread[2 * d, rows, :], spread[2 * d + 1, rows, :]], axis=1)
            spread16[d, k] = both.astype(BF16)
            return carry

        lax.fori_loop(0, 32, pack, 0, unroll=8)

        def route(k, carry):
            push(
                spread16.at[d, (w + k) % 32],
                routed.at[zh, w],
                route_send,
                route_recv,
                ((w + k) % 32, across * 2 + core),
            )
            return carry

        lax.fori_loop(1 - d, 32, route, 0)
    routed[zh, w] = spread16[0, w]

    kind = sub16 % 8
    late = (kind == 1) | (kind == 6)
    turns = (kind == 0) | (kind == 1) | (kind == 4) | (kind == 6)
    length = jnp.where(sub16 < 8, len_ref[0], len_ref[1])
    place_of = jnp.where(turns, length + jnp.where(late, 1, 0), 0).astype(F32)
    freqs = jnp.exp(-math.log(10000.0) * (lane16 % 64).astype(F32) * 2.0 / HEAD_DIM)
    angles = place_of * freqs
    cos = jnp.cos(angles)
    sin = jnp.where(lane16 < 64, -jnp.sin(angles), jnp.sin(angles))
    lane2 = lax.broadcasted_iota(jnp.int32, (16, 256), 1)
    sub2 = lax.broadcasted_iota(jnp.int32, (16, 256), 0)
    position = (lane2 % 128) // 2
    length2 = jnp.where(sub2 < 8, len_ref[0], len_ref[1])
    valid = (
        (lane2 % 2 == 0)
        & (lane2 // 128 == sub2 // 8)
        & ((position < length2) | (position == 62) | ((position == 63) & (sub2 % 8 == 1)))
    )
    inv = 1.0 / math.sqrt(HEAD_DIM)

    pltpu.make_async_copy(kv_raw, kv_raw, load_sem.at[6]).wait()
    kv = kv_raw.reshape(64, 256, 128)
    routed_all = routed.reshape(64, 16, 256)
    scales_ready()
    row_scale = jnp.zeros((16, 128), F32)
    for t in range(2):
        for j in range(2):
            here = scales[1, pl.ds(t * 8 + n * 2 + j, 1), :]
            own_rows = (sub16 == j * 8 + t) | (sub16 == j * 8 + 4 + 2 * t) | (sub16 == j * 8 + 5 + 2 * t)
            row_scale = jnp.where(own_rows, here, row_scale)
    drain(route_recv, routed_all.at[pl.ds(0, 63)])
    drain(route_send, routed_all.at[pl.ds(0, 63)])
    drain(core_send, zsend.at[1, pl.ds(0, 2)])

    def turn(k, carry):
        for hh in range(2):
            h = k * 2 + hh
            lanes = slice(hh * 128, hh * 128 + 128)
            vectors = total_of(routed[0, k, :, lanes], routed[1, k, :, lanes]) * row_scale
            vectors = vectors.astype(BF16).astype(F32)
            turned = vectors * cos + pltpu.roll(vectors, 64, axis=1) * sin
            turned16[h] = turned.astype(BF16)
            for j in range(2):
                old = kv[h, j * 128 + 112 : j * 128 + 128, :].astype(F32)
                fresh = jnp.where(sub8 >= 4, turned[j * 8 : j * 8 + 8], old[8:16])
                kv[h, j * 128 + 112 : j * 128 + 128, :] = jnp.concatenate([old[0:8], fresh], axis=0).astype(BF16)
        return carry

    lax.fori_loop(0, 32, turn, 0, unroll=4)

    def score(h, carry):
        scored[h] = dot_t(turned16[h], kv[h])
        return carry

    lax.fori_loop(0, 64, score, 0, unroll=8)

    def soften(h, carry):
        score = jnp.where(valid, scored[h] * inv, -1e30)
        grown = jnp.exp(score - jnp.max(score, axis=1, keepdims=True))
        weight = grown / jnp.sum(grown, axis=1, keepdims=True)
        weights16[h] = pltpu.roll(weight, 1, axis=1).astype(BF16)
        return carry

    lax.fori_loop(0, 64, soften, 0, unroll=8)

    def attend(k, carry):
        message = jnp.zeros((8, 128), F32)
        for hh in range(2):
            got = dot(weights16[k * 2 + hh], kv[k * 2 + hh])
            for j in range(2):
                at = hh * 4 + j * 2
                moved = pltpu.roll(got[j * 8 : j * 8 + 8], at, axis=0) if at else got[0:8]
                message = jnp.where((sub8 >= at) & (sub8 < at + 2), moved, message)
        att_send[k] = message.astype(BF16).astype(F32)
        return carry

    lax.fori_loop(0, 32, attend, 0, unroll=4)
    att_out_sem, att_in_sem = sems.sender(), sems.receiver()

    def spread_att(d, carry):
        push(att_send.at[(w + d) % 32], att_recv.at[zh, w], att_out_sem, att_in_sem, peer(d))
        return carry

    lax.fori_loop(1, 64, spread_att, 0)
    att_recv[zh, w] = att_send[w]
    att_all = att_recv.reshape(64, 8, 128)
    drain(att_in_sem, att_all.at[pl.ds(0, 63)])
    flat = att_recv.reshape(512, 128)
    swap_send, swap_recv = sems.sender(), sems.receiver()
    for m in range(2):
        for jt in range(4):
            for hh in range(2):
                piece = flat[pl.ds(m * 256 + hh * 4 + jt, 32, stride=8), :]
                piece = piece.astype(BF16).reshape(2, 16, 128)
                att_rows[m * 2 + core, jt * 2 : jt * 2 + 2, :, hh * 128 : hh * 128 + 128] = piece
        block = att_rows.at[m * 2 + core]
        push(block, block, swap_send, swap_recv, mate)
    drain(swap_recv, att_rows.at[pl.ds(0, 2)])
    drain(swap_send, att_rows.at[pl.ds(0, 2)])
    drain(att_out_sem, att_all.at[pl.ds(0, 63)])
    for m in range(4):
        for jt in range(4):
            j, t = jt // 2, jt % 2
            for hh in range(2):
                piece = att_rows[m, jt * 2 : jt * 2 + 2, :, hh * 128 : hh * 128 + 128].astype(F32)
                spread[hh, pl.ds(t * 8 + m * 2 + j, 32, stride=16), :] = piece.reshape(32, 128)

    def pack_rows(k, carry):
        rows = pl.ds(pl.multiple_of(k * 16, 16), 16)
        both = jnp.concatenate([spread[0, rows, :], spread[1, rows, :]], axis=1)
        att_full[k] = both.astype(BF16)
        return carry

    lax.fori_loop(0, 32, pack_rows, 0, unroll=8)
    loads[5].wait()

    def sink_out(p):
        def sink(total):
            cols = pl.ds(p * HALF, HALF)
            rows = (hidden1[p].astype(F32) + total).astype(BF16)
            out_ref[0, :, cols] = rows[0:8]
            out_ref[1, :, cols] = rows[8:16]

        return sink

    out_projection(1, att_full, attn_out, sink_out)
    modal_store.wait()
    pltpu.make_async_copy(fir_raw, fir_raw, load_sem.at[8]).wait()


def hand_over(a, b, c, out_a, out_b, out_c, held_a, held_b, held_c, sem):
    steps = ((a, held_a, out_a), (b, held_b, out_b), (c, held_c, out_c))
    ins = [pltpu.make_async_copy(src, held, sem.at[k]) for k, (src, held, _) in enumerate(steps)]
    outs = [pltpu.make_async_copy(held, dst, sem.at[3 + k]) for k, (_, held, dst) in enumerate(steps)]
    for copy in ins:
        copy.start()
    for copy_in, copy_out in zip(ins, outs):
        copy_in.wait()
        copy_out.start()
    for copy in outs:
        copy.wait()


def local(
    token_ids,
    lengths,
    embedding,
    hyena_gain,
    hyena_in,
    fir_taps,
    poles,
    residues,
    skip,
    hyena_out,
    modal_state,
    fir_state,
    attn_gain,
    attn_in,
    attn_out,
    kv_cache,
):
    vmem = pl.BlockSpec(memory_space=pltpu.VMEM)
    smem = pl.BlockSpec(memory_space=pltpu.SMEM)
    anywhere = pl.BlockSpec(memory_space=pl.ANY)
    out, modal_out, fir_out = pl.pallas_call(
        kernel,
        out_shape=(
            jax.ShapeDtypeStruct((2, 8, 2048), BF16),
            jax.ShapeDtypeStruct((64, 16, 256), F32),
            jax.ShapeDtypeStruct((64, 3, 2, 256), F32),
        ),
        in_specs=[smem] * 2 + [vmem] * 6 + [anywhere] * 8,
        out_specs=(vmem, anywhere, anywhere),
        scratch_shapes=[
            pltpu.VMEM((512, 2048), BF16),
            pltpu.VMEM((3, 2048, 256), BF16),
            pltpu.VMEM((64, 16, 256), F32),
            pltpu.VMEM((256, 2048), BF16),
            pltpu.VMEM((3, 2048, 256), BF16),
            pltpu.VMEM((256, 2048), BF16),
            pltpu.VMEM((64, 2, 64, 2, 128), BF16),
            pltpu.VMEM((6, 64, 2, 128), F32),
            pltpu.SemaphoreType.DMA((9,)),
            pltpu.SemaphoreType.DMA((16,)),
            pltpu.SemaphoreType.DMA((22,)),
            pltpu.SemaphoreType.DMA((2, 2, 9)),
            pltpu.SemaphoreType.DMA((2, 17)),
            pltpu.VMEM((32, 8, 128), jnp.int32),
            pltpu.VMEM((512, 2048), BF16),
            pltpu.VMEM((3, 512, 256), BF16),
            pltpu.VMEM((2, 4, 8, 16, 768), BF16),
            pltpu.VMEM((2, 2, 8, 16, 768), BF16),
            pltpu.VMEM((2, 8, 16, 768), BF16),
            pltpu.VMEM((2, 8, 16, 768), BF16),
            pltpu.VMEM((2, 16, 128), F32),
            pltpu.VMEM((2, 3, 16, 128), F32),
            pltpu.VMEM((2, 16, 128), F32),
            pltpu.VMEM((4, 8, 16, 256), BF16),
            pltpu.VMEM((2, 2, 32, 16, HALF), BF16),
            pltpu.VMEM((2, 2, 4, 2, 16, HALF), BF16),
            pltpu.VMEM((2, 2, 4, 4, 16, HALF), BF16),
            pltpu.VMEM((2, 2, 4, 2, 16, HALF), BF16),
            pltpu.VMEM((2, 2, 8, 16, HALF), BF16),
            pltpu.VMEM((2, 2, 8, 16, HALF), BF16),
            pltpu.VMEM((16, 2048), F32),
            pltpu.VMEM((2, 16, HALF), BF16),
            pltpu.VMEM((2, 32, 16, HALF), BF16),
            pltpu.VMEM((128, 768), F32),
            pltpu.VMEM((6, 512, 128), F32),
            pltpu.VMEM((4, 512, 128), F32),
            pltpu.VMEM((2, 32, 16, 256), BF16),
            pltpu.VMEM((2, 32, 16, 256), BF16),
            pltpu.VMEM((64, 16, 128), BF16),
            pltpu.VMEM((64, 16, 256), F32),
            pltpu.VMEM((64, 16, 256), BF16),
            pltpu.VMEM((32, 8, 128), F32),
            pltpu.VMEM((2, 32, 8, 128), F32),
            pltpu.VMEM((4, 8, 16, 256), BF16),
            pltpu.VMEM((32, 16, 256), BF16),
        ],
        compiler_params=pltpu.CompilerParams(
            collective_id=0, has_side_effects=True, vmem_limit_bytes=56 * 1024 * 1024
        ),
        name="decode",
    )(
        token_ids,
        lengths,
        hyena_gain[None, :],
        attn_gain[None, :],
        fir_taps,
        poles,
        residues,
        skip[None, :],
        fir_state.transpose(0, 2, 1, 3),
        embedding,
        hyena_in.transpose(1, 0, 2),
        modal_state,
        hyena_out,
        attn_in.transpose(1, 0, 2),
        attn_out,
        kv_cache,
    )
    made = (out, modal_out, fir_out)
    out, modal_out, fir_out = pl.pallas_call(
        hand_over,
        out_shape=[jax.ShapeDtypeStruct(array.shape, array.dtype) for array in made],
        in_specs=[anywhere] * 3,
        out_specs=[anywhere] * 3,
        scratch_shapes=[pltpu.VMEM(array.shape, array.dtype) for array in made]
        + [pltpu.SemaphoreType.DMA((6,))],
        name="hand_over",
    )(*made)
    return out, modal_out, fir_out.transpose(0, 2, 1, 3)


def solution(mesh):
    placed = (
        P(None, "wide"),
        P(("wide", "narrow")),
        P(None, "narrow"),
        P("narrow"),
        P("narrow", None, "wide"),
        P(None, None, "wide"),
        P(None, "wide"),
        P(None, "wide"),
        P("wide"),
        P("wide", "narrow"),
        P("narrow", None, "wide"),
        P("narrow", None, None, "wide"),
        P("narrow"),
        P("narrow", None, "wide"),
        P("wide", "narrow"),
        P(("wide", "narrow"), None, None, None),
    )
    return jax.shard_map(
        local,
        mesh=mesh,
        in_specs=placed,
        out_specs=(
            P(None, "wide", "narrow"),
            P("narrow", None, "wide"),
            P("narrow", None, None, "wide"),
        ),
        check_vma=False,
    )
```

time: 1460 us -> 122 us (0.08)
  waiting for transfers between devices: 1270 us -> 0 us
  Pallas kernels: 0 us -> 120 us
  blocking collectives: 69.2 us -> 0 us
  local copies, waits for them, and re-layouts: 43.1 us -> 0 us
  matrix products: 30.6 us -> 0 us
  starting transfers between devices: 15.1 us -> 0 us
    reduce_scatter x8 -> x0, waiting for transfers between devices: 680 us -> none  [the longest x2 310 us: local(): lax.psum_scatter(jnp.dot(mixer_all, hyena_out, preferred_element_type=jnp...]
    all_gather x4 -> x0, waiting for transfers between devices: 583 us -> none  [the longest x2 294 us: local(): lax.all_gather(normed0, 'wide', axis=0, tiled=True)]
    pallas_call x0 -> x2, Pallas kernels: none -> 120 us  [the longest x1 118 us: local(): pl.pallas_call(kernel, out_shape=(jax.ShapeDtypeStruct((2, 8, 2048), BF16...]
    dot_general x16 -> x0, matrix products: 30.6 us -> none  [the longest x2 8.28 us: local(): jnp.dot(lax.all_gather(normed1, 'wide', axis=0, tiled=True), qkv_matrix,...]
    all_gather x4 -> x0, blocking collectives: 27.7 us -> none  [the longest x2 13.9 us: local(): mixer_all = lax.all_gather(mixer, 'narrow', axis=0, tiled=True)]
    all_to_all x2 -> x0, blocking collectives: 23.5 us -> none  [local(): lax.all_to_all(pieces, 'wide', split_axis=1, concat_axis=0, tiled=True)]
    slice x2 -> x0, local copies, waits for them, and re-layouts: 22.9 us -> none  [the longest x1 21.9 us: attend_local(): keys = cache[:, :, 0].reshape(rows, span, HEADS, HEAD_DIM)]
    psum x2 -> x0, blocking collectives: 18 us -> none  [norm_rows(): total = lax.psum(jnp.sum(values * values, axis=1), 'narrow')]
  transfers between devices with their start and end apart: 14 -> 0, of which waited for: 13 -> 0; matrix products, arithmetic and copies ran while one was open for 5% -> 0% of each run, Pallas kernels for 0% -> 0%
where the time goes in v2:
time: 122 us; the launch traced here: 121 us
  Pallas kernels  120 us (98%)
    pallas_call x1, Pallas kernels, local(): pl.pallas_call(kernel, out_shape=(jax.ShapeDtypeStruct((2, 8, 2048), BF16...  118 us

profile of v2, /device:TPU:0, one launch (start us, length us, event | category | flops | bytes accessed | tf_op | source)
XLA Modules:
  0.0 120.8 jit_solution(1824474424537613726)
XLA Ops:
  0.6 117.8 %decode.1 = (bf16[2,8,2048]{2,1,0:T(8,128)(2,1)}, f32[64,16,256]{2,1,0:T(8,128)}, f32[64,3,2,256]{3,2,1,0:T(2,128)}) custom-call(s32[2,8]{1,0:T(2,128)} %tok_ref.1, s32[2]{0:T(128)} %len_ref.1, f32[1,2048]{1,0:T(1,128)} %bitcast.10, f32[1,2048]{1,0:T(1,128)} %bitcast.11, f32[3,3,256]{2,1,0:T(4,128)} %taps_ref.1, f32[16,256]{1,0:T(8,128)} %poles_ref.1, ...), custom_call_target="tpu_custom_call" | custom-call | tf_op jit(solution)/shard_map/decode/pallas_call | solution.py:799
  118.4 2.4 %hand_over.1 = (bf16[2,8,2048]{2,1,0:T(8,128)(2,1)}, f32[64,16,256]{2,1,0:T(8,128)}, f32[64,3,2,256]{3,2,1,0:T(2,128)}) custom-call(bf16[2,8,2048]{2,1,0:T(8,128)(2,1)} %get-tuple-element.9.a, f32[64,16,256]{2,1,0:T(8,128)} %get-tuple-element.10.b, f32[64,3,2,256]{3,2,1,0:T(2,128)} %get-tuple-element.11.c), custom_call_target="tpu_custom_call" | custom-call | tf_op jit(solution)/shard_map/hand_over/pallas_call | solution.py:878

commit v3 on v2

--- a/solution.py
+++ b/solution.py
@@ -1,3 +1,4 @@
+import functools
 import math
 
 import jax
@@ -97,25 +98,26 @@
     def block(step, h, o):
         return ((f + step) % 4) * 8 + zs[h] * 4 + (s + o) % 4
 
+    def close_of(h, o):
+        return close_sem.at[o if o or not h else 4]
+
     def hand_on(o):
         drain(far_sem.at[o], far.at[o])
         for h in (1, 0):
             temp[o, h] = total_of(src[block(steps[h], h, o)], far[o, h]).astype(BF16)
-            push(temp.at[o, h], close.at[o, h], send_sem, close_sem.at[o], place.along(first, steps[h]))
+            push(temp.at[o, h], close.at[o, h], send_sem, close_of(h, o), place.along(first, steps[h]))
 
     def send_close(o):
         for h in (1, 0):
             step = steps[1 - h]
-            push(src.at[block(step, h, o)], close.at[o, 2 + h], send_sem, close_sem.at[o], place.along(first, step))
-
-    def finish(o):
-        drain(close_sem.at[o], close.at[o])
-        for h in (1, 0):
-            total = total_of(src[block(0, h, o)], close[o, h], close[o, 2 + h])
-            if h or o:
-                mid[h * 4 + o] = total.astype(BF16)
-                there = place.shifted(second, o, h)
-                push(mid.at[h * 4 + o], inbox.at[h * 4 + o], send_sem, in_sem, there)
+            push(src.at[block(step, h, o)], close.at[o, 2 + h], send_sem, close_of(h, o), place.along(first, step))
+
+    def finish(h, o):
+        total = total_of(src[block(0, h, o)], close[o, h], close[o, 2 + h])
+        if h or o:
+            mid[h * 4 + o] = total.astype(BF16)
+            there = place.shifted(second, o, h)
+            push(mid.at[h * 4 + o], inbox.at[h * 4 + o], send_sem, in_sem, there)
         return total
 
     fill((f + 2) % 4)
@@ -138,13 +140,16 @@
     yield
     hand_on(0)
     yield
-    finish(2)
-    yield
-    finish(1)
-    finish(3)
-    yield
-    total = finish(0)
-    yield
+    for o in (2, 1, 3):
+        drain(close_sem.at[o], close.at[o])
+        finish(1, o)
+        finish(0, o)
+        yield
+    drain(close_sem.at[4], close.at[0, pl.ds(0, 2)])
+    finish(1, 0)
+    yield
+    drain(close_sem.at[0], close.at[0, pl.ds(0, 2)])
+    total = finish(0, 0)
     drain(in_sem, inbox.at[pl.ds(1, 7)])
     for k in range(1, 8):
         total = total + inbox[k].astype(F32)
@@ -152,20 +157,24 @@
     drain(send_sem, src.at[pl.ds(0, 31)])
 
 
-def ag_wide_part(place, sems, axes, held):
+def ag_wide_part(place, sems, axes, held, use):
     first, second = axes
     f, s = getattr(place, first), getattr(place, second)
     zs = (place.zl, 1 - place.zl)
     steps = (1, 3)
-    send_sem, in_sem, pass_sem, end_sem = sems
+    send_sem, in_sem, pass_sem, near_sem, end_sem = sems
 
     def block(step, h, o):
         return held.at[((f + step) % 4) * 8 + zs[h] * 4 + (s + o) % 4]
 
     def ring(h, o):
         for d, step in enumerate(steps):
-            sem = pass_sem.at[h * 4 + o] if d == h else end_sem
+            sem = pass_sem.at[h * 4 + o] if d == h else near_sem
             push(block(0, h, o), block(0, h, o), send_sem, sem, place.along(first, step))
+
+    def line(h):
+        for o in (1, 3, 2):
+            push(block(0, h, 0), block(0, h, 0), send_sem, in_sem.at[h * 4 + 4 - o], place.shifted(second, o, 0))
 
     def arrive(h, o):
         drain(in_sem.at[h * 4 + o], block(0, h, o))
@@ -176,35 +185,40 @@
         got = block(4 - steps[h], h, o)
         push(got, got, send_sem, end_sem, place.along(first, steps[h]))
 
-    own = block(0, 0, 0)
-    order = ((1, 0), (0, 1), (0, 3), (1, 1), (1, 3), (0, 2), (1, 2))
-    for h, o in order:
-        push(own, own, send_sem, in_sem.at[h * 4 + (4 - o) % 4], place.shifted(second, o, h))
-        if (h, o) == (0, 3):
-            ring(0, 0)
-    yield
-    arrive(1, 0)
+    push(block(0, 0, 0), block(0, 0, 0), send_sem, in_sem.at[4], place.shifted(second, 0, 1))
+    line(0)
+    ring(0, 0)
+    yield
+    drain(in_sem.at[4], block(0, 1, 0))
+    line(1)
+    ring(1, 0)
     yield
     arrive(0, 1)
     arrive(0, 3)
     yield
     pass_on(0, 0)
-    yield
+    arrive(0, 2)
+    yield
+    pass_on(1, 0)
     arrive(1, 1)
     arrive(1, 3)
     yield
-    pass_on(1, 0)
-    yield
-    arrive(0, 2)
     arrive(1, 2)
-    yield
-    for h, o in ((0, 1), (0, 3), (1, 1), (1, 3)):
+    pass_on(0, 1)
+    pass_on(0, 3)
+    yield
+    use(f)
+    yield
+    for h, o in ((0, 2), (1, 1), (1, 3), (1, 2)):
         pass_on(h, o)
     yield
-    for h, o in ((0, 2), (1, 2)):
-        pass_on(h, o)
-    yield
-    drain(end_sem, held.at[pl.ds(0, 16)])
+    drain(near_sem, held.at[pl.ds(0, 8)])
+    use((f + 1) % 4)
+    yield
+    use((f + 3) % 4)
+    yield
+    drain(end_sem, held.at[pl.ds(0, 8)])
+    use((f + 2) % 4)
     drain(send_sem, held.at[pl.ds(0, 31)])
 
 
@@ -246,19 +260,6 @@
         drain(cross_sem, z_recv.at[p])
     drain(send_sem, src.at[pl.ds(0, 3)])
     return [src.at[zh * 2 + c], core_recv.at[1], z_recv]
-
-
-def ag_narrow(place, sems, held):
-    zh, c = place.zh, place.c
-    own = held.at[place.n]
-    send_sem, cross_sem, core_sem = sems.sender(), sems.receiver(), sems.receiver()
-    push(own, own, send_sem, cross_sem, place.narrow(1, 0))
-    push(own, own, send_sem, core_sem, place.narrow(0, 1))
-    drain(cross_sem, own)
-    got = held.at[(1 - zh) * 2 + c]
-    push(got, got, send_sem, core_sem, place.narrow(0, 1))
-    drain(core_sem, held.at[pl.ds(0, 2)])
-    drain(send_sem, held.at[pl.ds(0, 3)])
 
 
 def share_scales(place, sems, sums, got, scales):
@@ -330,7 +331,11 @@
     held,
     qkv,
     wide_qkv,
-    spread,
+    qkv16,
+    route_pick,
+    att_pick,
+    rsend,
+    rcore,
     spread16,
     routed,
     turned16,
@@ -354,9 +359,9 @@
         pl.semaphore_signal(barrier, inc=1, device_id=peer(d), device_id_type=MESH)
         return carry
 
-    lax.fori_loop(1, 64, greet, 0)
-    for dzh in range(2):
-        pl.semaphore_signal(barrier, inc=1, device_id=place.narrow(dzh, 1), device_id_type=MESH)
+    lax.fori_loop(1, 32, greet, 0)
+    for dzh, dc in ((0, 1), (1, 0), (1, 1)):
+        pl.semaphore_signal(barrier, inc=1, device_id=place.narrow(dzh, dc), device_id_type=MESH)
 
     loads = []
     for k, (src, dst) in enumerate(
@@ -395,7 +400,7 @@
         push(tokens.at[w], tokens.at[w], token_send, token_recv, peer(d))
         return carry
 
-    pl.semaphore_wait(barrier, 65)
+    pl.semaphore_wait(barrier, 34)
     lax.fori_loop(1, 32, token_start, 0)
 
     lane16 = lax.broadcasted_iota(jnp.int32, (16, 128), 1)
@@ -432,17 +437,17 @@
 
     drain(token_recv, tokens.at[pl.ds(0, 31)])
     drain(token_send, tokens.at[pl.ds(0, 31)])
-    vocab = lax.broadcasted_iota(jnp.int32, (64, 512), 1)
+    vocab = lax.broadcasted_iota(jnp.int32, (128, 512), 1)
 
     def pick(m):
         rows = tokens[pl.ds(m * 8, 8)].reshape(64, 128)
-        for t in range(STEPS):
-            hot = (rows[:, t * 64 : t * 64 + 1] == vocab).astype(F32).astype(BF16)
-            for c in range(3):
-                picked = dot(hot, table[c]).astype(BF16).reshape(4, 16, 256)
-                zsend[0, m, t * 4 : t * 4 + 4, :, c * 256 : (c + 1) * 256] = picked
-
-    terms = rs_narrow(place, sems, zsend.at[0], pick, zcore.at[0], ztemp.at[0], zrecv.at[0])
+        column = jnp.concatenate([rows[:, 0:1], rows[:, 64:65]], axis=0)
+        hot = (column == vocab).astype(F32).astype(BF16)
+        for c in range(3):
+            picked = dot(hot, table[c]).astype(BF16).reshape(8, 16, 256)
+            zsend[m, :, :, c * 256 : (c + 1) * 256] = picked
+
+    terms = rs_narrow(place, sems, zsend, pick, zcore, ztemp, zrecv)
     scales_ready()
 
     own = tokens[w]
@@ -499,7 +504,12 @@
         return carry
 
     lax.fori_loop(0, 8, sum_terms, 0)
-    lax.fori_loop(0, 8, filters, 0)
+    mixer_send, mixer_recv = sems.sender(), sems.receiver()
+    for part in range(2):
+        lax.fori_loop(part * 4, part * 4 + 4, filters, 0, unroll=2)
+        done = mixers.at[n, pl.ds(part * 4, 4)]
+        for dzh, dc in ((1, 0), (1, 1), (0, 1)):
+            push(done, done, mixer_send, mixer_recv, place.narrow(dzh, dc))
     modal_store = pltpu.make_async_copy(modal, modal_out_hbm, load_sem.at[7])
     modal_store.start()
     for c in range(3):
@@ -507,7 +517,24 @@
             pltpu.make_async_copy(
                 fir_raw.at[c * 2 + half], fir_out_hbm.at[:, c, :, pl.ds(half * 128, 128)], load_sem.at[8]
             ).start()
-    ag_narrow(place, sems, mixers)
+
+    to_row = lax.broadcasted_iota(jnp.int32, (128, 384), 0)
+    from_row = lax.broadcasted_iota(jnp.int32, (128, 384), 1)
+    place_in = to_row % 8
+    branch = jnp.where(place_in < 2, 0, jnp.where(place_in < 4, 3, 1 + place_in % 2))
+    when = jnp.where(place_in < 2, place_in, (place_in - 4) // 2)
+    seen = (to_row // 16 == (from_row % 128) // 16) & (branch == from_row // 128)
+    for m in range(4):
+        hit = seen & (from_row % 16 == when * 8 + m * 2 + (to_row % 16) // 8)
+        route_pick[m] = jnp.where(hit, 1.0, 0.0).astype(BF16)
+    to_row = lax.broadcasted_iota(jnp.int32, (128, 256), 0)
+    from_row = lax.broadcasted_iota(jnp.int32, (128, 256), 1)
+    row = (from_row % 2) * 8 + (from_row // 64) * 2 + (from_row % 4) // 2
+    for hh in range(2):
+        hit = (to_row // 16 == (from_row % 64) // 8) & ((from_row % 8) // 4 == hh) & (to_row % 16 == row)
+        att_pick[hh] = jnp.where(hit, 1.0, 0.0).astype(BF16)
+    drain(mixer_recv, mixers.at[pl.ds(0, 3)])
+    drain(mixer_send, mixers.at[pl.ds(0, 3)])
 
     def out_projection(k, rows, weights, sink):
         def fill_a(y):
@@ -524,7 +551,7 @@
         for p, (axes, fill) in enumerate(((("y", "x"), fill_a), (("x", "y"), fill_b))):
             bufs = [b.at[k, p] for b in (far, close, temp, mid, inbox)]
             sem = rs_sem.at[k, p]
-            rs_sems = (sems.sender(), sem.at[pl.ds(0, 4)], sem.at[pl.ds(4, 4)], sem.at[8])
+            rs_sems = (sems.sender(), sem.at[pl.ds(0, 4)], sem.at[pl.ds(4, 5)], sem.at[9])
             gens.append(rs_wide_part(place, rs_sems, axes, psend.at[k, p], bufs, fill, sink(p)))
         interleave(*gens)
 
@@ -544,45 +571,41 @@
     squares = jnp.sum(total_of(hidden1[0]) ** 2 + total_of(hidden1[1]) ** 2, axis=1, keepdims=True)
     sums[1] = jnp.broadcast_to(squares, (16, 128))
     scales_ready = share_scales(place, sems, sums.at[1], sums_got.at[1], scales.at[1])
+    loads[4].wait()
+
+    def use_plane(p, plane):
+        gain = attn_gain_ref[:, p * HALF : (p + 1) * HALF]
+        rows = held[p, pl.ds(plane * 8, 8)].reshape(128, HALF).astype(F32) * gain
+        rows = rows.astype(BF16)
+        for c in range(3):
+            got = dot(rows, attn_in[c, p * HALF : (p + 1) * HALF, :])
+            if p == 0:
+                wide_qkv[0, c, pl.ds(pl.multiple_of(plane * 128, 128), 128), :] = got
+            else:
+                for k in range(8):
+                    at = pl.multiple_of(((k % 4) * 8 + (k // 4) * 4 + plane) * 16, 16)
+                    wide_qkv[1, c, pl.ds(at, 16), :] = got[k * 16 : k * 16 + 16]
+
     gens = []
     for p, axes in enumerate((("y", "x"), ("x", "y"))):
         sem = ag_sem.at[p]
-        ag_sems = (sems.sender(), sem.at[pl.ds(0, 8)], sem.at[pl.ds(8, 8)], sem.at[16])
-        gens.append(ag_wide_part(place, ag_sems, axes, held.at[p]))
+        ag_sems = (sems.sender(), sem.at[pl.ds(0, 8)], sem.at[pl.ds(8, 8)], sem.at[16], sem.at[17])
+        gens.append(ag_wide_part(place, ag_sems, axes, held.at[p], functools.partial(use_plane, p)))
     interleave(*gens)
 
-    loads[4].wait()
-
-    def gather_rows(k, carry):
-        a = held[0, k]
-        b = held[1, ((k % 4) * 2 + (k // 4) % 2) * 4 + k // 8]
-        both = jnp.concatenate([a, b], axis=1).astype(F32)
-        rows = pl.ds(pl.multiple_of(k * 16, 16), 16)
-        xg[rows, :] = (both * attn_gain_ref[...]).astype(BF16)
-        return carry
-
-    lax.fori_loop(0, 32, gather_rows, 0, unroll=4)
-
-    for c in range(3):
-
-        def project_qkv(m, carry):
-            rows = pl.ds(pl.multiple_of(m * 256, 256), 256)
-            got = dot(xg[rows, :], attn_in[c])
-            wide_qkv[2 * c, rows, :] = got[:, :128]
-            wide_qkv[2 * c + 1, rows, :] = got[:, 128:]
-            return carry
-
-        lax.fori_loop(0, 2, project_qkv, 0)
+    def join(k, carry):
+        rows = pl.ds(pl.multiple_of(k * 32, 32), 32)
+        for c in range(3):
+            both = wide_qkv[0, c, rows, :] + wide_qkv[1, c, rows, :]
+            qkv16[k // 4, pl.ds(pl.multiple_of(c * 128 + (k % 4) * 32, 32), 32), :] = both.astype(BF16)
+        return carry
+
+    lax.fori_loop(0, 16, join, 0, unroll=2)
 
     def split(m):
-        for t in range(2):
-            for j in range(2):
-                first = (t * 2 + j) * 2
-                for c in range(3):
-                    for half in range(2):
-                        piece = wide_qkv[2 * c + half, pl.ds(t * 8 + m * 2 + j, 32, stride=16), :]
-                        lanes = slice(c * 256 + half * 128, c * 256 + half * 128 + 128)
-                        zsend[1, m, first : first + 2, :, lanes] = piece.astype(BF16).reshape(2, 16, 128)
+        for g in range(4):
+            got = dot(route_pick[m], qkv16[g])
+            rsend[m, g * 8 : g * 8 + 8] = got.astype(BF16).reshape(8, 16, 256)
 
     zh, core = place.zh, place.c
     mate = place.narrow(0, 1)
@@ -592,29 +615,14 @@
     for d in (1, 0):
         half = (zh + d) % 2
         split(half * 2 + 1 - core)
-        push(zsend.at[1, half * 2 + 1 - core], zcore.at[1, half], core_send, core_recv[d], mate)
-    for half in range(2):
-        spread[half] = jnp.zeros((512, 128), F32)
-        spread[2 + half] = jnp.zeros((512, 128), F32)
+        push(rsend.at[half * 2 + 1 - core], rcore.at[half], core_send, core_recv[d], mate)
+    split((1 - zh) * 2 + core)
     for d in (1, 0):
         across = (zh + d) % 2
-        for tj in range(4):
-            t, j = tj // 2, tj % 2
-            if tj == 0:
-                split(across * 2 + core)
-                drain(core_recv[d], zcore.at[1, 0])
-            rows = slice(tj * 2, tj * 2 + 2)
-            total = total_of(zsend[1, across * 2 + core, rows], zcore[1, across, rows]).reshape(32, 768)
-            for c in range(3):
-                at = j * 8 + (t if c == 0 else 4 + 2 * t + (c - 1))
-                for half in range(2):
-                    lo = c * 256 + half * 128
-                    spread[2 * d + half, pl.ds(at, 32, stride=16), :] = total[:, lo : lo + 128]
+        drain(core_recv[d], rcore.at[0])
 
         def pack(k, carry):
-            rows = pl.ds(pl.multiple_of(k * 16, 16), 16)
-            both = jnp.concatenate([spread[2 * d, rows, :], spread[2 * d + 1, rows, :]], axis=1)
-            spread16[d, k] = both.astype(BF16)
+            spread16[d, k] = total_of(rsend[across * 2 + core, k], rcore[across, k]).astype(BF16)
             return carry
 
         lax.fori_loop(0, 32, pack, 0, unroll=8)
@@ -630,6 +638,8 @@
             return carry
 
         lax.fori_loop(1 - d, 32, route, 0)
+        if d:
+            split(zh * 2 + core)
     routed[zh, w] = spread16[0, w]
 
     kind = sub16 % 8
@@ -664,7 +674,7 @@
             row_scale = jnp.where(own_rows, here, row_scale)
     drain(route_recv, routed_all.at[pl.ds(0, 63)])
     drain(route_send, routed_all.at[pl.ds(0, 63)])
-    drain(core_send, zsend.at[1, pl.ds(0, 2)])
+    drain(core_send, rcore)
 
     def turn(k, carry):
         for hh in range(2):
@@ -691,7 +701,7 @@
     def soften(h, carry):
         score = jnp.where(valid, scored[h] * inv, -1e30)
         grown = jnp.exp(score - jnp.max(score, axis=1, keepdims=True))
-        weight = grown / jnp.sum(grown, axis=1, keepdims=True)
+        weight = grown * (1.0 / jnp.sum(grown, axis=1, keepdims=True))
         weights16[h] = pltpu.roll(weight, 1, axis=1).astype(BF16)
         return carry
 
@@ -719,33 +729,24 @@
     att_recv[zh, w] = att_send[w]
     att_all = att_recv.reshape(64, 8, 128)
     drain(att_in_sem, att_all.at[pl.ds(0, 63)])
-    flat = att_recv.reshape(512, 128)
     swap_send, swap_recv = sems.sender(), sems.receiver()
     for m in range(2):
-        for jt in range(4):
-            for hh in range(2):
-                piece = flat[pl.ds(m * 256 + hh * 4 + jt, 32, stride=8), :]
-                piece = piece.astype(BF16).reshape(2, 16, 128)
-                att_rows[m * 2 + core, jt * 2 : jt * 2 + 2, :, hh * 128 : hh * 128 + 128] = piece
+
+        def take(k, carry):
+            pair = att_recv[m, pl.ds(k * 2, 2)].reshape(16, 128)
+            att_rows[m * 2 + core, k] = pair.astype(BF16)
+            return carry
+
+        lax.fori_loop(0, 16, take, 0, unroll=8)
         block = att_rows.at[m * 2 + core]
         push(block, block, swap_send, swap_recv, mate)
     drain(swap_recv, att_rows.at[pl.ds(0, 2)])
     drain(swap_send, att_rows.at[pl.ds(0, 2)])
     drain(att_out_sem, att_all.at[pl.ds(0, 63)])
-    for m in range(4):
-        for jt in range(4):
-            j, t = jt // 2, jt % 2
-            for hh in range(2):
-                piece = att_rows[m, jt * 2 : jt * 2 + 2, :, hh * 128 : hh * 128 + 128].astype(F32)
-                spread[hh, pl.ds(t * 8 + m * 2 + j, 32, stride=16), :] = piece.reshape(32, 128)
-
-    def pack_rows(k, carry):
-        rows = pl.ds(pl.multiple_of(k * 16, 16), 16)
-        both = jnp.concatenate([spread[0, rows, :], spread[1, rows, :]], axis=1)
-        att_full[k] = both.astype(BF16)
-        return carry
-
-    lax.fori_loop(0, 32, pack_rows, 0, unroll=8)
+    for g in range(4):
+        stack = jnp.concatenate([att_rows[m, g * 4 : g * 4 + 4].reshape(64, 128) for m in range(4)], axis=0)
+        got = jnp.concatenate([dot(att_pick[hh], stack) for hh in range(2)], axis=1)
+        att_full[g * 8 : g * 8 + 8] = got.astype(BF16).reshape(8, 16, 256)
     loads[5].wait()
 
     def sink_out(p):
@@ -817,15 +818,15 @@
             pltpu.SemaphoreType.DMA((9,)),
             pltpu.SemaphoreType.DMA((16,)),
             pltpu.SemaphoreType.DMA((22,)),
-            pltpu.SemaphoreType.DMA((2, 2, 9)),
-            pltpu.SemaphoreType.DMA((2, 17)),
+            pltpu.SemaphoreType.DMA((2, 2, 10)),
+            pltpu.SemaphoreType.DMA((2, 18)),
             pltpu.VMEM((32, 8, 128), jnp.int32),
             pltpu.VMEM((512, 2048), BF16),
             pltpu.VMEM((3, 512, 256), BF16),
-            pltpu.VMEM((2, 4, 8, 16, 768), BF16),
-            pltpu.VMEM((2, 2, 8, 16, 768), BF16),
+            pltpu.VMEM((4, 8, 16, 768), BF16),
             pltpu.VMEM((2, 8, 16, 768), BF16),
-            pltpu.VMEM((2, 8, 16, 768), BF16),
+            pltpu.VMEM((8, 16, 768), BF16),
+            pltpu.VMEM((8, 16, 768), BF16),
             pltpu.VMEM((2, 16, 128), F32),
             pltpu.VMEM((2, 3, 16, 128), F32),
             pltpu.VMEM((2, 16, 128), F32),
@@ -840,8 +841,12 @@
             pltpu.VMEM((2, 16, HALF), BF16),
             pltpu.VMEM((2, 32, 16, HALF), BF16),
             pltpu.VMEM((128, 768), F32),
-            pltpu.VMEM((6, 512, 128), F32),
-            pltpu.VMEM((4, 512, 128), F32),
+            pltpu.VMEM((2, 3, 512, 256), F32),
+            pltpu.VMEM((4, 384, 256), BF16),
+            pltpu.VMEM((4, 128, 384), BF16),
+            pltpu.VMEM((2, 128, 256), BF16),
+            pltpu.VMEM((4, 32, 16, 256), BF16),
+            pltpu.VMEM((2, 32, 16, 256), BF16),
             pltpu.VMEM((2, 32, 16, 256), BF16),
             pltpu.VMEM((2, 32, 16, 256), BF16),
             pltpu.VMEM((64, 16, 128), BF16),
@@ -849,7 +854,7 @@
             pltpu.VMEM((64, 16, 256), BF16),
             pltpu.VMEM((32, 8, 128), F32),
             pltpu.VMEM((2, 32, 8, 128), F32),
-            pltpu.VMEM((4, 8, 16, 256), BF16),
+            pltpu.VMEM((4, 16, 16, 128), BF16),
             pltpu.VMEM((32, 16, 256), BF16),
         ],
         compiler_params=pltpu.CompilerParams(

time: 122 us -> 114 us (0.934)
  Pallas kernels: 120 us -> 113 us
    pallas_call x1, Pallas kernels: 118 us -> 110 us  [local(): pl.pallas_call(kernel, out_shape=(jax.ShapeDtypeStruct((2, 8, 2048), BF16...]
where the time goes in v3:
time: 114 us; the launch traced here: 113 us
  Pallas kernels  113 us (99%)
    pallas_call x1, Pallas kernels, local(): pl.pallas_call(kernel, out_shape=(jax.ShapeDtypeStruct((2, 8, 2048), BF16...  110 us
    pallas_call x1, Pallas kernels, local(): pl.pallas_call(hand_over, out_shape=[jax.ShapeDtypeStruct(array.shape, ar...  2.41 us

profile of v3, /device:TPU:0, one launch (start us, length us, event | category | flops | bytes accessed | tf_op | source)
XLA Modules:
  0.0 113.2 jit_solution(11756686673456555320)
XLA Ops:
  0.6 110.1 %decode.1 = (bf16[2,8,2048]{2,1,0:T(8,128)(2,1)}, f32[64,16,256]{2,1,0:T(8,128)}, f32[64,3,2,256]{3,2,1,0:T(2,128)}) custom-call(s32[2,8]{1,0:T(2,128)} %tok_ref.1, s32[2]{0:T(128)} %len_ref.1, f32[1,2048]{1,0:T(1,128)} %bitcast.10, f32[1,2048]{1,0:T(1,128)} %bitcast.11, f32[3,3,256]{2,1,0:T(4,128)} %taps_ref.1, f32[16,256]{1,0:T(8,128)} %poles_ref.1, ...), custom_call_target="tpu_custom_call" | custom-call | tf_op jit(solution)/shard_map/decode/pallas_call | solution.py:800
  110.8 2.4 %hand_over.1 = (bf16[2,8,2048]{2,1,0:T(8,128)(2,1)}, f32[64,16,256]{2,1,0:T(8,128)}, f32[64,3,2,256]{3,2,1,0:T(2,128)}) custom-call(bf16[2,8,2048]{2,1,0:T(8,128)(2,1)} %get-tuple-element.9.a, f32[64,16,256]{2,1,0:T(8,128)} %get-tuple-element.10.b, f32[64,3,2,256]{3,2,1,0:T(2,128)} %get-tuple-element.11.c), custom_call_target="tpu_custom_call" | custom-call | tf_op jit(solution)/shard_map/hand_over/pallas_call | solution.py:883

commit v4 on v3

--- a/solution.py
+++ b/solution.py
@@ -88,8 +88,8 @@
 
 
 def rs_wide_part(place, sems, axes, src, bufs, fill, out):
-    far, close, temp, mid, inbox = bufs
-    send_sem, far_sem, close_sem, in_sem = sems
+    far, close, temp, mid, inbox, over = bufs
+    send_sem, far_sem, close_sem, in_sem, over_sem = sems
     first, second = axes
     f, s = getattr(place, first), getattr(place, second)
     zs = (place.zl, 1 - place.zl)
@@ -98,61 +98,70 @@
     def block(step, h, o):
         return ((f + step) % 4) * 8 + zs[h] * 4 + (s + o) % 4
 
-    def close_of(h, o):
-        return close_sem.at[o if o or not h else 4]
+    def cross(step):
+        fill((f + step) % 4)
+        push(src.at[block(step, 1, 0)], over.at[step], send_sem, over_sem.at[step], place.along("zl", 1))
+
+    def crossed(step):
+        drain(over_sem.at[step], over.at[step])
+        return total_of(src[block(step, 0, 0)], over[step])
 
     def hand_on(o):
         drain(far_sem.at[o], far.at[o])
         for h in (1, 0):
             temp[o, h] = total_of(src[block(steps[h], h, o)], far[o, h]).astype(BF16)
-            push(temp.at[o, h], close.at[o, h], send_sem, close_of(h, o), place.along(first, steps[h]))
+            push(temp.at[o, h], close.at[o, h], send_sem, close_sem.at[o], place.along(first, steps[h]))
 
     def send_close(o):
         for h in (1, 0):
             step = steps[1 - h]
-            push(src.at[block(step, h, o)], close.at[o, 2 + h], send_sem, close_of(h, o), place.along(first, step))
-
-    def finish(h, o):
-        total = total_of(src[block(0, h, o)], close[o, h], close[o, 2 + h])
-        if h or o:
+            push(src.at[block(step, h, o)], close.at[o, 2 + h], send_sem, close_sem.at[o], place.along(first, step))
+
+    cross(2)
+    for o in (2, 1, 3):
+        for h in (1, 0):
+            push(src.at[block(2, h, o)], far.at[o, h], send_sem, far_sem.at[o], place.along(first, steps[h]))
+    yield
+    cross(1)
+    cross(3)
+    send_close(2)
+    yield
+    hand_on(2)
+    send_close(1)
+    send_close(3)
+    yield
+    temp[0, 0] = crossed(2).astype(BF16)
+    push(temp.at[0, 0], far.at[0, 0], send_sem, far_sem.at[0], place.along(first, 1))
+    yield
+    cross(0)
+    yield
+    hand_on(1)
+    hand_on(3)
+    yield
+    temp[0, 1] = crossed(3).astype(BF16)
+    push(temp.at[0, 1], close.at[0, 2], send_sem, close_sem.at[0], place.along(first, 3))
+    yield
+    for o in (2, 1, 3):
+        if o == 2:
+            drain(far_sem.at[0], far.at[0, 0])
+            mid[0] = (crossed(1) + far[0, 0].astype(F32)).astype(BF16)
+            push(mid.at[0], close.at[0, 0], send_sem, close_sem.at[0], place.along(first, 1))
+            yield
+        drain(close_sem.at[o], close.at[o])
+        for h in (1, 0):
+            total = total_of(src[block(0, h, o)], close[o, h], close[o, 2 + h])
             mid[h * 4 + o] = total.astype(BF16)
             there = place.shifted(second, o, h)
             push(mid.at[h * 4 + o], inbox.at[h * 4 + o], send_sem, in_sem, there)
-        return total
-
-    fill((f + 2) % 4)
-    for o in (2, 1, 3, 0):
-        for h in (1, 0):
-            push(src.at[block(2, h, o)], far.at[o, h], send_sem, far_sem.at[o], place.along(first, steps[h]))
-    yield
-    fill((f + 1) % 4)
-    fill((f + 3) % 4)
-    send_close(2)
-    yield
-    hand_on(2)
-    send_close(1)
-    send_close(3)
-    yield
-    fill(f)
-    hand_on(1)
-    hand_on(3)
-    send_close(0)
-    yield
-    hand_on(0)
-    yield
-    for o in (2, 1, 3):
-        drain(close_sem.at[o], close.at[o])
-        finish(1, o)
-        finish(0, o)
         yield
-    drain(close_sem.at[4], close.at[0, pl.ds(0, 2)])
-    finish(1, 0)
-    yield
+    total = crossed(0)
     drain(close_sem.at[0], close.at[0, pl.ds(0, 2)])
-    total = finish(0, 0)
-    drain(in_sem, inbox.at[pl.ds(1, 7)])
-    for k in range(1, 8):
-        total = total + inbox[k].astype(F32)
+    total = total + close[0, 0].astype(F32) + close[0, 2].astype(F32)
+    yield
+    drain(in_sem, inbox.at[pl.ds(0, 6)])
+    for h in range(2):
+        for o in (1, 2, 3):
+            total = total + inbox[h * 4 + o].astype(F32)
     out(total)
     drain(send_sem, src.at[pl.ds(0, 31)])
 
@@ -326,6 +335,7 @@
     temp,
     mid,
     inbox,
+    over,
     hidden0,
     hidden1,
     held,
@@ -506,7 +516,7 @@
     lax.fori_loop(0, 8, sum_terms, 0)
     mixer_send, mixer_recv = sems.sender(), sems.receiver()
     for part in range(2):
-        lax.fori_loop(part * 4, part * 4 + 4, filters, 0, unroll=2)
+        lax.fori_loop(part * 4, part * 4 + 4, filters, 0, unroll=4)
         done = mixers.at[n, pl.ds(part * 4, 4)]
         for dzh, dc in ((1, 0), (1, 1), (0, 1)):
             push(done, done, mixer_send, mixer_recv, place.narrow(dzh, dc))
@@ -549,9 +559,9 @@
 
         gens = []
         for p, (axes, fill) in enumerate(((("y", "x"), fill_a), (("x", "y"), fill_b))):
-            bufs = [b.at[k, p] for b in (far, close, temp, mid, inbox)]
+            bufs = [b.at[k, p] for b in (far, close, temp, mid, inbox, over)]
             sem = rs_sem.at[k, p]
-            rs_sems = (sems.sender(), sem.at[pl.ds(0, 4)], sem.at[pl.ds(4, 5)], sem.at[9])
+            rs_sems = (sems.sender(), sem.at[pl.ds(0, 4)], sem.at[pl.ds(4, 4)], sem.at[8], sem.at[pl.ds(9, 4)])
             gens.append(rs_wide_part(place, rs_sems, axes, psend.at[k, p], bufs, fill, sink(p)))
         interleave(*gens)
 
@@ -818,7 +828,7 @@
             pltpu.SemaphoreType.DMA((9,)),
             pltpu.SemaphoreType.DMA((16,)),
             pltpu.SemaphoreType.DMA((22,)),
-            pltpu.SemaphoreType.DMA((2, 2, 10)),
+            pltpu.SemaphoreType.DMA((2, 2, 13)),
             pltpu.SemaphoreType.DMA((2, 18)),
             pltpu.VMEM((32, 8, 128), jnp.int32),
             pltpu.VMEM((512, 2048), BF16),
@@ -837,6 +847,7 @@
             pltpu.VMEM((2, 2, 4, 2, 16, HALF), BF16),
             pltpu.VMEM((2, 2, 8, 16, HALF), BF16),
             pltpu.VMEM((2, 2, 8, 16, HALF), BF16),
+            pltpu.VMEM((2, 2, 4, 16, HALF), BF16),
             pltpu.VMEM((16, 2048), F32),
             pltpu.VMEM((2, 16, HALF), BF16),
             pltpu.VMEM((2, 32, 16, HALF), BF16),

time: 114 us -> 110 us (0.965)
  Pallas kernels: 113 us -> 110 us
    pallas_call x1, Pallas kernels: 110 us -> 107 us  [local(): pl.pallas_call(kernel, out_shape=(jax.ShapeDtypeStruct((2, 8, 2048), BF16...]
where the time goes in v4:
time: 110 us
  Pallas kernels  110 us (100%)
    pallas_call x1, Pallas kernels, local(): pl.pallas_call(kernel, out_shape=(jax.ShapeDtypeStruct((2, 8, 2048), BF16...  107 us
    pallas_call x1, Pallas kernels, local(): pl.pallas_call(hand_over, out_shape=[jax.ShapeDtypeStruct(array.shape, ar...  2.41 us

profile of v4, /device:TPU:0, one launch (start us, length us, event | category | flops | bytes accessed | tf_op | source)
XLA Modules:
  0.0 110.2 jit_solution(13746596088250952513)
XLA Ops:
  0.6 107.1 %decode.1 = (bf16[2,8,2048]{2,1,0:T(8,128)(2,1)}, f32[64,16,256]{2,1,0:T(8,128)}, f32[64,3,2,256]{3,2,1,0:T(2,128)}) custom-call(s32[2,8]{1,0:T(2,128)} %tok_ref.1, s32[2]{0:T(128)} %len_ref.1, f32[1,2048]{1,0:T(1,128)} %bitcast.10, f32[1,2048]{1,0:T(1,128)} %bitcast.11, f32[3,3,256]{2,1,0:T(4,128)} %taps_ref.1, f32[16,256]{1,0:T(8,128)} %poles_ref.1, ...), custom_call_target="tpu_custom_call" | custom-call | tf_op jit(solution)/shard_map/decode/pallas_call | solution.py:810
  107.8 2.4 %hand_over.1 = (bf16[2,8,2048]{2,1,0:T(8,128)(2,1)}, f32[64,16,256]{2,1,0:T(8,128)}, f32[64,3,2,256]{3,2,1,0:T(2,128)}) custom-call(bf16[2,8,2048]{2,1,0:T(8,128)(2,1)} %get-tuple-element.9.a, f32[64,16,256]{2,1,0:T(8,128)} %get-tuple-element.10.b, f32[64,3,2,256]{3,2,1,0:T(2,128)} %get-tuple-element.11.c), custom_call_target="tpu_custom_call" | custom-call | tf_op jit(solution)/shard_map/hand_over/pallas_call | solution.py:894

commit v5 on v4

--- a/solution.py
+++ b/solution.py
@@ -717,25 +717,30 @@
 
     lax.fori_loop(0, 64, soften, 0, unroll=8)
 
-    def attend(k, carry):
-        message = jnp.zeros((8, 128), F32)
-        for hh in range(2):
-            got = dot(weights16[k * 2 + hh], kv[k * 2 + hh])
-            for j in range(2):
-                at = hh * 4 + j * 2
-                moved = pltpu.roll(got[j * 8 : j * 8 + 8], at, axis=0) if at else got[0:8]
-                message = jnp.where((sub8 >= at) & (sub8 < at + 2), moved, message)
-        att_send[k] = message.astype(BF16).astype(F32)
-        return carry
-
-    lax.fori_loop(0, 32, attend, 0, unroll=4)
     att_out_sem, att_in_sem = sems.sender(), sems.receiver()
+
+    def attend(i, carry):
+        tiles = [(w + i * 4 + u) % 32 for u in range(4)]
+        for k in tiles:
+            message = jnp.zeros((8, 128), F32)
+            for hh in range(2):
+                got = dot(weights16[k * 2 + hh], kv[k * 2 + hh])
+                for j in range(2):
+                    at = hh * 4 + j * 2
+                    moved = pltpu.roll(got[j * 8 : j * 8 + 8], at, axis=0) if at else got[0:8]
+                    message = jnp.where((sub8 >= at) & (sub8 < at + 2), moved, message)
+            att_send[k] = message.astype(BF16).astype(F32)
+        for k in tiles:
+            push(att_send.at[k], att_recv.at[zh, w], att_out_sem, att_in_sem, (k, (1 - zh) * 2 + core))
+        return carry
+
+    lax.fori_loop(0, 8, attend, 0)
 
     def spread_att(d, carry):
         push(att_send.at[(w + d) % 32], att_recv.at[zh, w], att_out_sem, att_in_sem, peer(d))
         return carry
 
-    lax.fori_loop(1, 64, spread_att, 0)
+    lax.fori_loop(1, 32, spread_att, 0)
     att_recv[zh, w] = att_send[w]
     att_all = att_recv.reshape(64, 8, 128)
     drain(att_in_sem, att_all.at[pl.ds(0, 63)])

time: 110 us -> 108 us (0.982)
  Pallas kernels: 110 us -> 107 us
    pallas_call x1, Pallas kernels: 107 us -> 105 us  [local(): pl.pallas_call(kernel, out_shape=(jax.ShapeDtypeStruct((2, 8, 2048), BF16...]
where the time goes in v5:
time: 108 us
  Pallas kernels  107 us (99%)
    pallas_call x1, Pallas kernels, local(): pl.pallas_call(kernel, out_shape=(jax.ShapeDtypeStruct((2, 8, 2048), BF16...  105 us
    pallas_call x1, Pallas kernels, local(): pl.pallas_call(hand_over, out_shape=[jax.ShapeDtypeStruct(array.shape, ar...  2.41 us

profile of v5, /device:TPU:0, one launch (start us, length us, event | category | flops | bytes accessed | tf_op | source)
XLA Modules:
  0.0 107.7 jit_solution(10272520942625443176)
XLA Ops:
  0.6 104.7 %decode.1 = (bf16[2,8,2048]{2,1,0:T(8,128)(2,1)}, f32[64,16,256]{2,1,0:T(8,128)}, f32[64,3,2,256]{3,2,1,0:T(2,128)}) custom-call(s32[2,8]{1,0:T(2,128)} %tok_ref.1, s32[2]{0:T(128)} %len_ref.1, f32[1,2048]{1,0:T(1,128)} %bitcast.10, f32[1,2048]{1,0:T(1,128)} %bitcast.11, f32[3,3,256]{2,1,0:T(4,128)} %taps_ref.1, f32[16,256]{1,0:T(8,128)} %poles_ref.1, ...), custom_call_target="tpu_custom_call" | custom-call | tf_op jit(solution)/shard_map/decode/pallas_call | solution.py:815
  105.3 2.4 %hand_over.1 = (bf16[2,8,2048]{2,1,0:T(8,128)(2,1)}, f32[64,16,256]{2,1,0:T(8,128)}, f32[64,3,2,256]{3,2,1,0:T(2,128)}) custom-call(bf16[2,8,2048]{2,1,0:T(8,128)(2,1)} %get-tuple-element.9.a, f32[64,16,256]{2,1,0:T(8,128)} %get-tuple-element.10.b, f32[64,3,2,256]{3,2,1,0:T(2,128)} %get-tuple-element.11.c), custom_call_target="tpu_custom_call" | custom-call | tf_op jit(solution)/shard_map/hand_over/pallas_call | solution.py:899
